TPU v7x, 512 devices: a whole 4x8x8 slice. The times are simulated.
512 devices in a mesh: seq: 32 (over z_hi, y, core), tensor: 16 (over x, z_lo).
Axes of the slice: x: 4, y: 8, z: 8 (z_hi: 2, z_lo: 4; z = z_hi * 4 + z_lo), core: 2. Of those that a mesh axis runs over, the one named last changes fastest.
Arguments:
- hidden_in: bfloat16 [8192, 5376], P('seq', 'tensor'), may hold values from -128 to 128
- positions: int32 [8192], P('seq'), may hold values from 0 to 16382, as said below
- pre_gain: float32 [5376], replicated, may hold values from -0.5 to 1.5
- query_weight: bfloat16 [5376, 4096], P('seq', 'tensor')
- key_weight: bfloat16 [5376, 2048], P('seq', 'tensor')
- value_weight: bfloat16 [5376, 2048], P('seq', 'tensor'), may hold values from -0.078125 to 0.078125
- query_gain: float32 [128], replicated, may hold values from -0.3 to 4.5
- key_gain: float32 [128], replicated, may hold values from -0.3 to 4.5
- output_weight: bfloat16 [4096, 5376], P('tensor', 'seq')
- post_gain: float32 [5376], P('tensor'), may hold values from -0.5 to 1.5
Outputs:
- hidden_out: bfloat16 [8192, 5376], P('seq', 'tensor')
Inputs may be any that keep to these rules, and one draw needn't show every extreme that they name: `positions`: 0 at a prompt's first token, else one more than the position of the token before; the window's first token continues a prompt begun before the window, and some later token starts a new prompt.
All inputs are finite; a program needn't handle non-finite values.
Results may differ from a plain program's by a relative error of at most 0.013.
Values may be sent and summed in bfloat16 or wider, within the bound.
A program may use at most 64 MiB of HBM per device.

v0:
```python
import jax
import jax.numpy as jnp
from jax import lax
from jax.sharding import PartitionSpec as P

WINDOW = 1024


epsilon = 1e-06
query_scalar = 168.0
rope_base = 10000.0
masked_score = -1e30


def passed_along(value, axis, steps):
    count = lax.axis_size(axis)
    initial, last = (max(0, -steps), min(count, count - steps))
    return lax.ppermute(value, axis, [(source, source + steps) for source in range(initial, last)])


def rms_scale(values):
    return values * lax.rsqrt(jnp.mean(values * values, axis=-1, keepdims=True) + epsilon)


def rotary(values, token_positions):
    half_dim = values.shape[-1] // 2
    exponent = jnp.arange(half_dim, dtype=jnp.float32) * 2.0 / values.shape[-1]
    inverse = 1.0 / rope_base**exponent
    angles = token_positions.astype(jnp.float32)[:, None] * inverse[None, :]
    cosine = jnp.cos(angles)[:, None, :]
    sine = jnp.sin(angles)[:, None, :]
    first_half = values[..., :half_dim]
    second_half = values[..., half_dim:]
    return jnp.concatenate(
        [first_half * cosine - second_half * sine, second_half * cosine + first_half * sine],
        axis=-1,
    )


def body(
    hidden_in,
    positions,
    pre_gain,
    query_weight,
    key_weight,
    value_weight,
    query_gain,
    key_gain,
    output_weight,
    post_gain,
):
    tokens_dev = hidden_in.shape[0]
    width_dev = hidden_in.shape[1]
    head_dim = query_gain.shape[0]
    kv_local = key_weight.shape[1] // head_dim
    whole = lax.all_gather(hidden_in, "tensor", axis=1, tiled=True)
    normed = (rms_scale(whole.astype(jnp.float32)) * (1.0 + pre_gain)).astype(jnp.bfloat16)

    def accumulate(piece):
        return jnp.dot(normed, piece, preferred_element_type=jnp.float32)

    query_sum = accumulate(lax.all_gather(query_weight, "seq", axis=0, tiled=True))
    key_sum = accumulate(lax.all_gather(key_weight, "seq", axis=0, tiled=True))
    value_sum = accumulate(lax.all_gather(value_weight, "seq", axis=0, tiled=True))
    queries = rotary(
        rms_scale(query_sum.reshape(tokens_dev, -1, head_dim)) * (1.0 + query_gain), positions
    )
    queries = queries.astype(jnp.bfloat16).reshape(tokens_dev, kv_local, 2, head_dim)
    key_own = rotary(
        rms_scale(key_sum.reshape(tokens_dev, kv_local, head_dim)) * (1.0 + key_gain), positions
    ).astype(jnp.bfloat16)
    value_own = value_sum.reshape(tokens_dev, kv_local, head_dim).astype(jnp.bfloat16)
    reach = (WINDOW + tokens_dev - 2) // tokens_dev
    earlier = []
    for distance in range(reach, 0, -1):
        earlier.append(passed_along((key_own, value_own), "seq", distance))
    key_rows = jnp.concatenate([pair[0] for pair in earlier] + [key_own], axis=0)
    value_rows = jnp.concatenate([pair[1] for pair in earlier] + [value_own], axis=0)
    seq_index = lax.axis_index("seq")
    query_index = seq_index * tokens_dev + jnp.arange(tokens_dev, dtype=jnp.int32)
    key_index = (seq_index - reach) * tokens_dev + jnp.arange(key_rows.shape[0], dtype=jnp.int32)
    gap = query_index[:, None] - key_index[None, :]
    allowed = (gap >= 0) & (gap < WINDOW) & (gap <= positions[:, None]) & (key_index >= 0)[None, :]
    scores = jnp.einsum(
        "qgrd,kgd->grqk", queries, key_rows, preferred_element_type=jnp.float32
    ) * query_scalar ** (-0.5)
    scores = jnp.where(allowed[None, None], scores, masked_score)
    peak = jnp.max(scores, axis=-1, keepdims=True)
    expo = jnp.exp(scores - peak)
    weights = (expo / jnp.sum(expo, axis=-1, keepdims=True)).astype(jnp.bfloat16)
    context = jnp.einsum("grqk,kgd->qgrd", weights, value_rows, preferred_element_type=jnp.float32)
    context = context.astype(jnp.bfloat16).reshape(tokens_dev, -1)
    term = jnp.dot(
        context,
        lax.all_gather(output_weight, "seq", axis=1, tiled=True),
        preferred_element_type=jnp.float32,
    )
    share = lax.psum_scatter(
        term.astype(jnp.bfloat16), "tensor", scatter_dimension=1, tiled=True
    ).astype(jnp.float32)
    squares = lax.psum(jnp.sum(share * share, axis=-1), "tensor")
    mean_square = squares / (width_dev * lax.axis_size("tensor"))
    post = share * lax.rsqrt(mean_square[:, None] + epsilon) * (1.0 + post_gain)
    return (hidden_in.astype(jnp.float32) + post).astype(jnp.bfloat16)


def solution(mesh):
    placed = (
        P("seq", "tensor"),
        P("seq"),
        P(),
        P("seq", "tensor"),
        P("seq", "tensor"),
        P("seq", "tensor"),
        P(),
        P(),
        P("tensor", "seq"),
        P("tensor"),
    )
    return jax.shard_map(
        body, mesh=mesh, in_specs=placed, out_specs=P("seq", "tensor"), check_vma=False
    )
```

profile of v0, /device:TPU:6, one launch (start us, length us, event | category | flops | bytes accessed | tf_op | source)
XLA Modules:
  0.0 614.7 jit_solution(4040736795534656457)
XLA Ops:
  6.5 0.7 all-gather.6.cloned.1.call-update
  7.3 0.7 all-gather.10.cloned.1.call-update
  10.0 0.7 broadcast_add_fusion
  13.3 1.6 fusion.10
  14.9 86.8 %all-gather.6.cloned.1.call-done = bf16[256,5376]{0,1:T(8,128)(2,1)} async-done(((bf16[256,336]{0,1:T(8,128)(2,1)}), bf16[256,5376]{0,1:T(8,128)(2,1)}) %all-gather.6.cloned.1.call-update) | async-done | bytes 2752528 | tf_op jit(solution)/shard_map/all_gather | solution.py:56
  101.8 2.7 fusion
  104.5 94.5 %all-gather.10.cloned.1.call-done = bf16[5376,128]{1,0:T(8,128)(2,1)} async-done(((bf16[168,128]{1,0:T(8,128)(2,1)}), bf16[5376,128]{1,0:T(8,128)(2,1)}) %all-gather.10.cloned.1.call-update) | async-done | bytes 1376272 | tf_op jit(solution)/shard_map/all_gather | solution.py:63
  199.0 2.7 multiply_reduce_fusion.1
  202.2 4.0 collective-permute-start.4
  206.2 3.4 collective-permute-start.5
  209.5 3.0 collective-permute-start.6
  212.5 2.4 collective-permute-start.7
  214.9 72.7 %all-gather.8.cloned.1.call-done = bf16[5376,128]{1,0:T(8,128)(2,1)} async-done(((bf16[168,128]{1,0:T(8,128)(2,1)}), bf16[5376,128]{1,0:T(8,128)(2,1)}) %all-gather.8.cloned.1.call-update) | async-done | bytes 1376272 | tf_op jit(solution)/shard_map/all_gather | solution.py:64
  287.6 3.1 fusion.14
  290.7 3.3 collective-permute-start
  294.1 2.7 collective-permute-start.1
  296.8 1.5 constant_dynamic-update-slice_fusion.9
  298.3 3.0 collective-permute-start.2
  301.3 1.5 constant_dynamic-update-slice_fusion.8
  302.8 3.0 collective-permute-start.3
  305.8 1.5 constant_dynamic-update-slice_fusion.7
  311.8 71.4 %all-gather.12.cloned.1.call-done = bf16[5376,256]{1,0:T(8,128)(2,1)} async-done(((bf16[168,256]{1,0:T(8,128)(2,1)}), bf16[5376,256]{1,0:T(8,128)(2,1)}) %all-gather.12.cloned.1.call-update) | async-done | bytes 2752528 | tf_op jit(solution)/shard_map/all_gather | solution.py:62
  383.1 4.2 multiply_reduce_fusion
  387.3 1.1 copy.11
  388.7 1.6 fusion.38
  390.7 1.6 fusion.11
  392.3 85.6 %all-gather.14.cloned.1.call-done = bf16[256,5376]{0,1:T(8,128)(2,1)} async-done(((bf16[256,168]{0,1:T(8,128)(2,1)}), bf16[256,5376]{0,1:T(8,128)(2,1)}) %all-gather.14.cloned.1.call-update) | async-done | bytes 2752528 | tf_op jit(solution)/shard_map/all_gather | solution.py:95
  477.9 4.2 convolution_convert_fusion
  482.8 83.3 %reduce-scatter.2.cloned.1.call-done = bf16[256,336]{0,1:T(8,128)(2,1)} async-done(((bf16[256,5376]{0,1:T(8,128)(2,1)}), bf16[256,336]{0,1:T(8,128)(2,1)}) %reduce-scatter.2.cloned.1.call-update) | async-done | bytes 172048 | tf_op jit(solution)/shard_map/reduce_scatter | solution.py:98
  566.1 1.0 fusion.15
  567.1 39.0 %psum.7 = f32[256]{0:T(256)S(1)} all-reduce(f32[256]{0:T(256)S(1)} %fusion.15), channel_id=1, replica_groups=mesh['seq'=32,'tensor'=16] {'tensor'}, use_global_device_ids=true, to_apply=%region_7.8 | all-reduce | flops 256 | bytes 2048 | tf_op jit(solution)/shard_map/psum | solution.py:101
  606.2 1.7 fusion.18
  (52 shorter events, 10.8 us)
Async XLA Ops:
  6.5 95.2 %all-gather.6.cloned.1.call-start = ((), (), s32[]{:S(2)}) async-start(), calls=%async_computation.1 | async-start | bytes 2924544 | tf_op jit(solution)/shard_map/all_gather | solution.py:56
  7.3 191.7 %all-gather.10.cloned.1.call-start = ((), (), s32[]{:S(2)}) async-start(), calls=%async_computation.3 | async-start | bytes 1419264 | tf_op jit(solution)/shard_map/all_gather | solution.py:63
  8.0 279.6 %all-gather.8.cloned.1.call-start = ((), (), s32[]{:S(2)}) async-start(), calls=%async_computation.2 | async-start | bytes 1419264 | tf_op jit(solution)/shard_map/all_gather | solution.py:64
  8.7 374.4 %all-gather.12.cloned.1.call-start = ((), (), s32[]{:S(2)}) async-start(), calls=%async_computation.4 | async-start | bytes 2838528 | tf_op jit(solution)/shard_map/all_gather | solution.py:62
  9.3 468.6 %all-gather.14.cloned.1.call-start = ((), (), s32[]{:S(2)}) async-start(), calls=%async_computation.5 | async-start | bytes 2838528 | tf_op jit(solution)/shard_map/all_gather | solution.py:95
  9.9 556.2 %reduce-scatter.2.cloned.1.call-start = ((), (), s32[]{:S(2)}) async-start(), calls=%async_computation.6 | async-start | bytes 2924544 | tf_op jit(solution)/shard_map/reduce_scatter | solution.py:98
  10.7 191.0 %copy-start.2 = (f32[5376]{0:T(1024)}, f32[5376]{0:T(1024)S(1)}, u32[]{:S(2)}) copy-start(f32[5376]{0:T(1024)S(1)} %broadcast_add_fusion) | copy-start | bytes 64516
  101.8 97.2 %copy-start = (bf16[256,5376]{0,1:T(8,128)(2,1)S(1)}, bf16[256,5376]{0,1:T(8,128)(2,1)}, u32[]{:S(2)}) copy-start(bf16[256,5376]{0,1:T(8,128)(2,1)} %all-gather.6.cloned.1.call-done) | copy-start | bytes 8257540
  202.2 91.9 %collective-permute-start.4 = (bf16[256,1,128]{0,2,1:T(8,128)(2,1)S(1)}, bf16[256,1,128]{0,2,1:T(8,128)(2,1)}, u32[]{:S(2)}, u32[]{:S(2)}) collective-permute-start(bf16[256,1,128]{0,2,1:T(8,128)(2,1)S(1)} %pad_maximum_fusion), channel_id=1, source_target_pairs={{0,64},{16,80},{32,96},{48,112},{64,128},{80,144},{96,160},{112,17... | collective-permute-start | bytes 196616 | tf_op jit(solution)/shard_map/ppermute | solution.py:18
  206.2 92.1 %collective-permute-start.5 = (bf16[256,1,128]{0,2,1:T(8,128)(2,1)S(1)}, bf16[256,1,128]{0,2,1:T(8,128)(2,1)}, u32[]{:S(2)}, u32[]{:S(2)}) collective-permute-start(bf16[256,1,128]{0,2,1:T(8,128)(2,1)S(1)} %pad_maximum_fusion), channel_id=1, source_target_pairs={{0,48},{16,64},{32,80},{48,96},{64,112},{80,128},{96,144},{112,160... | collective-permute-start | bytes 196616 | tf_op jit(solution)/shard_map/ppermute | solution.py:18
  209.5 93.3 %collective-permute-start.6 = (bf16[256,1,128]{0,2,1:T(8,128)(2,1)S(1)}, bf16[256,1,128]{0,2,1:T(8,128)(2,1)}, u32[]{:S(2)}, u32[]{:S(2)}) collective-permute-start(bf16[256,1,128]{0,2,1:T(8,128)(2,1)S(1)} %pad_maximum_fusion), channel_id=1, source_target_pairs={{0,32},{16,48},{32,64},{48,80},{64,96},{80,112},{96,128},{112,144}... | collective-permute-start | bytes 196616 | tf_op jit(solution)/shard_map/ppermute | solution.py:18
  212.5 94.7 %collective-permute-start.7 = (bf16[256,1,128]{0,2,1:T(8,128)(2,1)S(1)}, bf16[256,1,128]{0,2,1:T(8,128)(2,1)S(1)}, u32[]{:S(2)}, u32[]{:S(2)}) collective-permute-start(bf16[256,1,128]{0,2,1:T(8,128)(2,1)S(1)} %pad_maximum_fusion), channel_id=1, source_target_pairs={{0,16},{16,32},{32,48},{48,64},{64,80},{80,96},{96,112},{112,128},... | collective-permute-start | bytes 196616 | tf_op jit(solution)/shard_map/ppermute | solution.py:18
  290.7 17.9 %collective-permute-start = (bf16[256,1,128]{2,0,1:T(8,128)(2,1)S(1)}, bf16[256,1,128]{2,0,1:T(8,128)(2,1)S(1)}, u32[]{:S(2)}, u32[]{:S(2)}) collective-permute-start(bf16[256,1,128]{2,0,1:T(8,128)(2,1)S(1)} %fusion.14), channel_id=1, source_target_pairs={{0,64},{16,80},{32,96},{48,112},{64,128},{80,144},{96,160},{112,17... | collective-permute-start | bytes 196616 | tf_op jit(solution)/shard_map/ppermute | solution.py:18
  294.1 15.1 %collective-permute-start.1 = (bf16[256,1,128]{2,0,1:T(8,128)(2,1)S(1)}, bf16[256,1,128]{2,0,1:T(8,128)(2,1)S(1)}, u32[]{:S(2)}, u32[]{:S(2)}) collective-permute-start(bf16[256,1,128]{2,0,1:T(8,128)(2,1)S(1)} %fusion.14), channel_id=1, source_target_pairs={{0,48},{16,64},{32,80},{48,96},{64,112},{80,128},{96,144},{112,160... | collective-permute-start | bytes 196616 | tf_op jit(solution)/shard_map/ppermute | solution.py:18
  298.3 11.6 %collective-permute-start.2 = (bf16[256,1,128]{2,0,1:T(8,128)(2,1)S(1)}, bf16[256,1,128]{2,0,1:T(8,128)(2,1)S(1)}, u32[]{:S(2)}, u32[]{:S(2)}) collective-permute-start(bf16[256,1,128]{2,0,1:T(8,128)(2,1)S(1)} %fusion.14), channel_id=1, source_target_pairs={{0,32},{16,48},{32,64},{48,80},{64,96},{80,112},{96,128},{112,144}... | collective-permute-start | bytes 196616 | tf_op jit(solution)/shard_map/ppermute | solution.py:18
  302.8 7.7 %collective-permute-start.3 = (bf16[256,1,128]{2,0,1:T(8,128)(2,1)S(1)}, bf16[256,1,128]{2,0,1:T(8,128)(2,1)S(1)}, u32[]{:S(2)}, u32[]{:S(2)}) collective-permute-start(bf16[256,1,128]{2,0,1:T(8,128)(2,1)S(1)} %fusion.14), channel_id=1, source_target_pairs={{0,16},{16,32},{32,48},{48,64},{64,80},{80,96},{96,112},{112,128},... | collective-permute-start | bytes 196616 | tf_op jit(solution)/shard_map/ppermute | solution.py:18
  482.2 0.7 copy-start.3
  482.2 124.0 %copy-start.1 = (bf16[256,336]{0,1:T(8,128)(2,1)S(1)}, bf16[256,336]{0,1:T(8,128)(2,1)}, u32[]{:S(2)}) copy-start(bf16[256,336]{0,1:T(8,128)(2,1)} %param.10) | copy-start | bytes 516100
Sparse Core Ops, SparseCore 0:
  9.4 92.3 all-gather.5
  105.0 93.9 all-gather.9
  202.2 85.3 all-gather.7
  290.7 92.3 all-gather.11
  386.2 91.6 all-gather.13
  482.3 83.7 reduce-scatter.1
where the time goes:
time: 624 us; the launch traced here: 615 us
  waiting for transfers between devices  497 us (80%)
  blocking collectives  39 us (6%)
  starting transfers between devices  25.1 us (4%)
  matrix products  17.4 us (3%)
  between operations  13.7 us (2%)
  other arithmetic  12 us (2%)
  local copies, waits for them, and re-layouts  10 us (2%)
    all_gather x1, waiting for transfers between devices, body(): key_sum = accumulate(lax.all_gather(key_weight, 'seq', axis=0, tiled=True))  94.5 us
    all_gather x1, waiting for transfers between devices, body(): whole = lax.all_gather(hidden_in, 'tensor', axis=1, tiled=True)  86.8 us
    all_gather x1, waiting for transfers between devices, body(): lax.all_gather(output_weight, 'seq', axis=1, tiled=True)  85.6 us
    reduce_scatter x1, waiting for transfers between devices, body(): lax.psum_scatter(term.astype(jnp.bfloat16), 'tensor', scatter_dimension=1...  83.3 us
    all_gather x1, waiting for transfers between devices, body(): lax.all_gather(value_weight, 'seq', axis=0, tiled=True)  72.7 us
    all_gather x1, waiting for transfers between devices, body(): lax.all_gather(query_weight, 'seq', axis=0, tiled=True)  71.4 us
    psum x1, blocking collectives, body(): squares = lax.psum(jnp.sum(share * share, axis=-1), 'tensor')  39 us
    ppermute x8, starting transfers between devices, passed_along(): lax.ppermute(value, axis, [(source, source + steps) for source in range(i...  24.9 us
  transfers between devices with their start and end apart: 14, of which 6 were waited for; matrix products, arithmetic and copies ran while one was open for 5% of the time, Pallas kernels for 0%

commit v1 on v0

v1 whole, which is shorter than its diff:
```python
import jax
import jax.numpy as jnp
from jax import lax
from jax.experimental import pallas as pl
from jax.experimental.pallas import tpu as pltpu
from jax.sharding import PartitionSpec as P

D = 5376
HEAD_DIM = 128
WINDOW = 1024
FEAT = 336
HALF = 168
TOK = 256
EPS = 1e-6
SCORE_SCALE = 168.0**-0.5
LOG2E = 1.4426950408889634
MESH = pl.DeviceIdType.MESH
F32 = jnp.float32
BF16 = jnp.bfloat16

REACH = ((4, 3), (3, 4))


def kernel(
    h_ref,
    pos_ref,
    gain_ref,
    wq_ref,
    wk_ref,
    wv_ref,
    qg_ref,
    kg_ref,
    wo_ref,
    pg_ref,
    inv_ref,
    out_ref,
    xg,
    xt,
    wb,
    ws,
    tmp,
    cst,
    kv,
    qb,
    ctx,
    acc,
    sq,
    trig,
    oacc,
    zpart,
    xpart,
    zs,
    zr,
    xs,
    xr,
    rs,
    rr,
    ps,
    pr,
    bs,
    br,
    ms,
    mr,
    hs,
    hr,
    qs,
    qr,
    loc,
):
    s = lax.axis_index("seq")
    t = lax.axis_index("tensor")
    core = lax.rem(s, 2)
    c = s // 2
    y = lax.rem(c, 8)
    zh = c // 8
    x = t // 4
    zl = lax.rem(t, 4)
    other = 1 - core

    def at_seq(chip, which):
        return {"seq": chip * 2 + which, "tensor": t}

    def at_tensor(xx, zz):
        return {"seq": s, "tensor": lax.rem(xx + 8, 4) * 4 + zz}

    sibling = at_seq(c, other)
    far_half = at_seq((1 - zh) * 8 + y, core)
    y_up = at_seq(zh * 8 + lax.rem(y + 1, 8), core)
    y_down = at_seq(zh * 8 + lax.rem(y + 7, 8), core)
    next_chip = at_seq(lax.rem(c + 1, 16), core)
    prev_chip = at_seq(lax.rem(c + 15, 16), core)
    mirror = {"seq": t * 2 + core, "tensor": c}
    off_diagonal = c != t

    pending = []

    def send(src, dst, ssem, rsem, dev, cond=None):
        copy = pltpu.make_async_remote_copy(
            src_ref=src, dst_ref=dst, send_sem=ssem, recv_sem=rsem, device_id=dev, device_id_type=MESH
        )
        if cond is None:
            copy.start()
        else:
            pl.when(cond)(copy.start)
        pending.append((copy, cond))

    def recv(dst, ssem, rsem, cond=None):
        copy = pltpu.make_async_remote_copy(
            src_ref=dst, dst_ref=dst, send_sem=ssem, recv_sem=rsem, device_id=sibling, device_id_type=MESH
        )
        if cond is None:
            copy.wait_recv()
        else:
            pl.when(cond)(copy.wait_recv)

    barrier = pltpu.get_barrier_semaphore()
    peers = [sibling, far_half, y_up, y_down, next_chip, prev_chip]
    peers += [at_tensor(x + d, zl) for d in (1, 2, 3)]
    peers += [at_tensor(x, lax.rem(zl + d, 4)) for d in (1, 2, 3)]
    for peer in peers:
        pl.semaphore_signal(barrier, inc=1, device_id=peer, device_id_type=MESH)

    @pl.when(off_diagonal)
    def _():
        pl.semaphore_signal(barrier, inc=1, device_id=mirror, device_id_type=MESH)

    xg[t] = h_ref[...]
    gain = 1.0 + gain_ref[...]
    ws[0] = (wk_ref[...].astype(F32) * gain).astype(BF16)
    ws[1] = (wv_ref[...].astype(F32) * gain).astype(BF16)
    ws[2] = (wq_ref[:, 0:128].astype(F32) * gain).astype(BF16)
    ws[3] = (wq_ref[:, 128:256].astype(F32) * gain).astype(BF16)
    ws[4] = wo_ref[:, 0:128]
    ws[5] = wo_ref[:, 128:256]

    pl.semaphore_wait(barrier, jnp.where(off_diagonal, len(peers) + 1, len(peers)))

    def near_z(n):
        if n == 0:
            return zl
        if n == 1:
            return zl + 1 - 2 * lax.rem(zl, 2)
        if n == 2:
            return 2 - zl // 2
        return 3 * (1 - zl // 2)

    class TensorFlow:
        def __init__(self, buf, k):
            self.buf = buf
            self.k = k

        def slot(self, dx, n):
            return lax.rem(x + dx + 4, 4) * 4 + near_z(n)

        def to_x(self, n):
            blk = self.buf.at[self.slot(0, n)]
            for i, d in enumerate((1, -1)):
                send(blk, blk, xs.at[self.k, n, i], xr.at[self.k, n, i], at_tensor(x + d, zl))

        def own(self):
            self.to_x(0)
            blk = self.buf.at[self.slot(0, 0)]
            send(blk, blk, zs.at[self.k, 0], zr.at[self.k, zl], at_tensor(x, lax.rem(zl + 1, 4)), zl < 3)
            send(blk, blk, zs.at[self.k, 4], zr.at[self.k, zl], at_tensor(x, lax.rem(zl + 3, 4)), zl > 0)

        def on_z(self, n):
            q = near_z(n)
            blk = self.buf.at[self.slot(0, n)]
            recv(blk, zs.at[self.k, n], zr.at[self.k, q])
            up = q < zl
            ok = jnp.where(up, zl < 3, zl > 0)
            dev = at_tensor(x, jnp.where(up, lax.rem(zl + 1, 4), lax.rem(zl + 3, 4)))
            send(blk, blk, zs.at[self.k, n], zr.at[self.k, q], dev, ok)
            self.to_x(n)

        def on_x(self, n):
            d = 1 - 2 * lax.rem(core + n, 2)
            for i, dx in enumerate((-1, 1)):
                recv(self.buf.at[self.slot(dx, n)], xs.at[self.k, n, i], xr.at[self.k, n, i])
            blk = self.buf.at[self.slot(-d, n)]
            send(blk, blk, xs.at[self.k, n, 2], xr.at[self.k, n, 2], at_tensor(x + d, zl))

        def on_far(self, n):
            recv(self.buf.at[self.slot(2, n)], xs.at[self.k, n, 2], xr.at[self.k, n, 2])

    def w_slot(part, way, d):
        half = zh if part == 0 else 1 - zh
        yy = lax.rem(y + (8 - d if way == 0 else d), 8)
        return half * 8 + yy

    def ring_send(k, part, way, d):
        if d < REACH[part][way]:
            blk = wb.at[2 * k + core, w_slot(part, way, d)]
            i = (part * 2 + way) * 4 + d
            send(blk, blk, rs.at[k, i], rr.at[k, i], y_up if way == 0 else y_down)

    def relay(k, j):
        blk = wb.at[2 * k + core, j]
        send(blk, blk, bs.at[k, j], br.at[k, j], sibling)

    def on_ring(k, part, way, d):
        j = w_slot(part, way, d)
        i = (part * 2 + way) * 4 + d - 1
        recv(wb.at[2 * k + core, j], rs.at[k, i], rr.at[k, i])
        ring_send(k, part, way, d)
        relay(k, j)

    def on_rings(k, part, d):
        for way in (0, 1):
            if d <= REACH[part][way]:
                on_ring(k, part, way, d)

    def own_ring(k):
        own = wb.at[2 * k + core, c]
        send(own, own, ps.at[k, 1], pr.at[k, 1], far_half)
        for way in (0, 1):
            ring_send(k, 0, way, 0)
        relay(k, c)

    def on_half(k):
        j = (1 - zh) * 8 + y
        recv(wb.at[2 * k + core, j], ps.at[k, 1], pr.at[k, 1])
        for way in (0, 1):
            ring_send(k, 1, way, 0)
        relay(k, j)

    def swapped(k):
        recv(tmp.at[k], ps.at[k, 0], pr.at[k, 0])
        mine = ws[2 * k + core].astype(F32)
        theirs = tmp[k].astype(F32)
        low = jnp.where(core == 0, mine, theirs)
        high = jnp.where(core == 0, theirs, mine)
        return jnp.concatenate([low, high], axis=0).astype(BF16)

    hidden = TensorFlow(xg, 0)
    for k in range(3):
        send(ws.at[2 * k + other], tmp.at[k], ps.at[k, 0], pr.at[k, 0], sibling)
    hidden.own()
    for k in range(2):
        wb[2 * k + core, c] = swapped(k)
        own_ring(k)
    cst[...] = swapped(2)

    pos_wide = jnp.transpose(jnp.broadcast_to(pos_ref[...].astype(F32), (HEAD_DIM, TOK)))
    angles = pos_wide * inv_ref[...]
    lane = lax.broadcasted_iota(jnp.int32, (TOK, HEAD_DIM), 1)
    trig[0] = jnp.cos(angles)
    sine = jnp.sin(angles)
    trig[1] = jnp.where(lane < HEAD_DIM // 2, -sine, sine)

    sq[...] = jnp.zeros_like(sq)

    def take(j):
        block = xg[j].astype(F32)
        xt[j] = jnp.transpose(block).astype(BF16)
        sq[0:1, :] += jnp.sum(block * block, axis=0, keepdims=True)

    def on_x(n):
        hidden.on_x(n)
        take(hidden.slot(-1, n))
        take(hidden.slot(1, n))

    def on_z(n):
        hidden.on_z(n)
        take(hidden.slot(0, n))

    def on_far(n):
        hidden.on_far(n)
        take(hidden.slot(2, n))

    take(t)
    on_rings(0, 0, 1)
    on_x(0)
    on_z(1)
    on_rings(1, 0, 1)
    on_rings(0, 0, 2)
    on_half(0)
    on_z(2)
    on_rings(1, 0, 2)
    on_far(0)
    on_half(1)
    on_x(1)
    on_rings(0, 1, 1)
    on_rings(0, 0, 3)
    on_z(3)
    on_rings(1, 0, 3)
    on_rings(0, 1, 2)
    on_far(1)
    on_x(2)
    on_rings(1, 1, 1)
    on_rings(0, 0, 4)
    on_rings(1, 1, 2)
    on_rings(0, 1, 3)
    on_far(2)
    on_x(3)

    send(cst, wb.at[4 + core, t], ms.at[0], mr.at[0], mirror, off_diagonal)

    @pl.when(jnp.logical_not(off_diagonal))
    def _():
        local = pltpu.make_async_copy(cst, wb.at[4 + core, c], loc)
        local.start()
        local.wait()

    on_rings(1, 0, 4)
    on_rings(1, 1, 3)
    on_rings(0, 1, 4)
    on_far(3)

    mean_sq = jnp.transpose(jnp.broadcast_to(sq[0:1, :], (HEAD_DIM, TOK))) / D
    recv(wb.at[4 + core, c], ms.at[0], mr.at[0], off_diagonal)
    own_ring(2)

    def project(k):
        acc[...] = jnp.zeros_like(acc)

        def step(j, carry):
            recv(wb.at[2 * k + other, j], bs.at[k, j], br.at[k, j])
            both = jnp.concatenate([wb[2 * k, j], wb[2 * k + 1, j]], axis=1)
            acc[...] += jnp.dot(xt[j], both, preferred_element_type=F32)
            return carry

        lax.fori_loop(0, 16, step, 0)

    def head(raw, gain_row):
        mean = jnp.mean(raw * raw, axis=-1, keepdims=True)
        unit = raw * lax.rsqrt(mean + EPS * (mean_sq + EPS)) * (1.0 + gain_row)
        return unit * trig[0] + pltpu.roll(unit, HEAD_DIM // 2, 1) * trig[1]

    project(0)
    kv[4, 0] = head(acc[:, 0:128], kg_ref[...]).astype(BF16)
    kv[4, 1] = (acc[:, 128:256] * lax.rsqrt(mean_sq + EPS)).astype(BF16)

    send(kv.at[4], kv.at[2], hs.at[0], hr.at[2], next_chip, c < 15)
    send(kv.at[4], kv.at[3], hs.at[2], hr.at[3], sibling, core == 0)
    for i in range(4):

        @pl.when(s + i < 4)
        def _():
            kv[i] = jnp.zeros((2, TOK, HEAD_DIM), BF16)

    on_rings(1, 1, 4)
    on_half(2)
    on_rings(2, 0, 1)
    project(1)
    recv(kv.at[2], hs.at[0], hr.at[2], c >= 1)
    send(kv.at[2], kv.at[0], hs.at[1], hr.at[0], next_chip, jnp.logical_and(c >= 1, c < 15))
    send(kv.at[2], kv.at[1 + 2 * core], hs.at[3], hr.at[1 + 2 * core], sibling, c >= 1)
    for i in range(2):
        qb[i] = head(acc[:, i * 128 : (i + 1) * 128], qg_ref[...]).astype(BF16)
    on_rings(2, 0, 2)
    on_rings(2, 1, 1)
    recv(kv.at[0], hs.at[1], hr.at[0], c >= 2)
    send(kv.at[0], kv.at[1], hs.at[4], hr.at[1], sibling, jnp.logical_and(c >= 2, core == 1))
    recv(kv.at[3], hs.at[2], hr.at[3], s >= 1)
    on_rings(2, 0, 3)
    on_rings(2, 1, 2)
    recv(kv.at[1], hs.at[3], hr.at[1], s >= 3)

    ROWS = 128

    def attend(step, carry):
        r = lax.rem(step, 2)
        hd = step // 2
        rows = pl.ds(pl.multiple_of(r * ROWS, ROWS), ROWS)
        query = qb[hd, rows, :]
        position = jnp.transpose(jnp.broadcast_to(pos_ref[...], (HEAD_DIM, TOK)).astype(F32)[:, 0:ROWS])
        position = jnp.where(
            r == 0,
            position,
            jnp.transpose(jnp.broadcast_to(pos_ref[...], (HEAD_DIM, TOK)).astype(F32)[:, ROWS:TOK]),
        ).astype(jnp.int32)
        position = jnp.concatenate([position, position], axis=1)
        row = lax.broadcasted_iota(jnp.int32, (ROWS, TOK), 0) + r * ROWS
        col = lax.broadcasted_iota(jnp.int32, (ROWS, TOK), 1)
        limit = jnp.minimum(jnp.minimum(position, row + s * TOK), WINDOW - 1)
        scores = []
        for i in range(5):
            raw = lax.dot_general(query, kv[i, 0], (((1,), (1,)), ((), ())), preferred_element_type=F32)
            gap = row + (4 - i) * TOK - col
            allowed = gap <= limit
            if i == 4:
                allowed = jnp.logical_and(allowed, gap >= 0)
            scores.append(jnp.where(allowed, raw, -1e30))
        peak = scores[0]
        for i in range(1, 5):
            peak = jnp.maximum(peak, scores[i])
        peak = jnp.max(peak, axis=-1, keepdims=True)
        total = jnp.zeros((ROWS, TOK), F32)
        mixed = jnp.zeros((ROWS, HEAD_DIM), F32)
        for i in range(5):
            expo = jnp.exp2((scores[i] - peak) * (SCORE_SCALE * LOG2E))
            total += expo
            mixed += jnp.dot(expo.astype(BF16), kv[i, 1], preferred_element_type=F32)
        mixed = mixed / jnp.sum(total, axis=-1, keepdims=True)
        ctx[t, hd, rows, :] = mixed.astype(BF16)
        return carry

    lax.fori_loop(0, 4, attend, 0)

    context = TensorFlow(ctx, 1)
    context.own()
    on_rings(2, 0, 4)
    on_rings(2, 1, 3)
    on_rings(2, 1, 4)

    def wait_out(j, carry):
        recv(wb.at[4 + other, j], bs.at[2, j], br.at[2, j])
        return carry

    lax.fori_loop(0, 16, wait_out, 0)
    oacc[...] = jnp.zeros_like(oacc)

    def out_step(j):
        left = jnp.concatenate([wb[4, j], wb[5, j]], axis=1)
        right = jnp.concatenate([ctx[j, 0], ctx[j, 1]], axis=1)
        oacc[...] += lax.dot_general(left, right, (((1,), (1,)), ((), ())), preferred_element_type=F32)

    def c_x(n):
        context.on_x(n)
        out_step(context.slot(-1, n))
        out_step(context.slot(1, n))

    def c_z(n):
        context.on_z(n)
        out_step(context.slot(0, n))

    def c_far(n):
        context.on_far(n)
        out_step(context.slot(2, n))

    out_step(t)
    c_z(1)
    c_x(0)
    c_z(2)
    c_x(1)
    c_far(0)
    c_z(3)
    c_x(2)
    c_far(1)
    c_x(3)
    c_far(2)
    c_far(3)

    def spread(buf, k, me, device):
        for i, d in enumerate((1, 2, 3)):
            send(buf.at[me], buf.at[me], qs.at[k, i], qr.at[k, me], device(lax.rem(me + d, 4)))
        for d in (1, 2, 3):
            j = lax.rem(me + d, 4)
            recv(buf.at[j], qs.at[k, d - 1], qr.at[k, j])
        return buf[0] + buf[1] + buf[2] + buf[3]

    attention = oacc[...]
    zpart[zl] = jnp.broadcast_to(jnp.sum(attention * attention, axis=0, keepdims=True), (8, TOK))
    xpart[x] = spread(zpart, 0, zl, lambda j: at_tensor(x, j))
    squares = spread(xpart, 1, x, lambda j: at_tensor(j, zl))
    scale = lax.rsqrt(squares[0:1, :] / D + EPS)
    post = oacc[...] * scale * (1.0 + pg_ref[...])
    out_ref[...] = (h_ref[...].astype(F32) + post).astype(BF16)

    for copy, cond in pending:
        if cond is None:
            copy.wait_send()
        else:
            pl.when(cond)(copy.wait_send)


def body(
    hidden_in,
    positions,
    pre_gain,
    query_weight,
    key_weight,
    value_weight,
    query_gain,
    key_gain,
    output_weight,
    post_gain,
):
    s = lax.axis_index("seq")
    exponent = jnp.arange(HEAD_DIM // 2, dtype=F32) * 2.0 / HEAD_DIM
    inverse = 1.0 / 10000.0**exponent
    inverse = jnp.concatenate([inverse, inverse])[None, :]
    gain = lax.dynamic_slice(pre_gain, (s * HALF,), (HALF,)).reshape(HALF, 1)
    vmem = pl.BlockSpec(memory_space=pltpu.VMEM)
    dma = pltpu.SemaphoreType.DMA
    out = pl.pallas_call(
        kernel,
        out_shape=jax.ShapeDtypeStruct((FEAT, TOK), BF16),
        in_specs=[vmem] * 11,
        out_specs=vmem,
        scratch_shapes=[
            pltpu.VMEM((16, FEAT, TOK), BF16),
            pltpu.VMEM((16, TOK, FEAT), BF16),
            pltpu.VMEM((6, 16, FEAT, 128), BF16),
            pltpu.VMEM((6, HALF, 128), BF16),
            pltpu.VMEM((3, HALF, 128), BF16),
            pltpu.VMEM((FEAT, 128), BF16),
            pltpu.VMEM((5, 2, TOK, HEAD_DIM), BF16),
            pltpu.VMEM((2, TOK, HEAD_DIM), BF16),
            pltpu.VMEM((16, 2, TOK, HEAD_DIM), BF16),
            pltpu.VMEM((TOK, 256), F32),
            pltpu.VMEM((8, TOK), F32),
            pltpu.VMEM((2, TOK, HEAD_DIM), F32),
            pltpu.VMEM((FEAT, TOK), F32),
            pltpu.VMEM((4, 8, TOK), F32),
            pltpu.VMEM((4, 8, TOK), F32),
            dma((2, 5)),
            dma((2, 4)),
            dma((2, 4, 3)),
            dma((2, 4, 3)),
            dma((3, 16)),
            dma((3, 16)),
            dma((3, 2)),
            dma((3, 2)),
            dma((3, 16)),
            dma((3, 16)),
            dma((1,)),
            dma((1,)),
            dma((5,)),
            dma((5,)),
            dma((2, 3)),
            dma((2, 4)),
            dma,
        ],
        compiler_params=pltpu.CompilerParams(
            collective_id=0, has_side_effects=True, vmem_limit_bytes=56 << 20
        ),
        cost_estimate=pl.CostEstimate(flops=3_000_000_000, bytes_accessed=1_000_000, transcendentals=1_000_000),
    )(
        hidden_in.T,
        positions[None, :],
        gain,
        query_weight,
        key_weight,
        value_weight,
        query_gain[None, :],
        key_gain[None, :],
        output_weight.T,
        post_gain[:, None],
        inverse,
    )
    return out.T


def solution(mesh):
    placed = (
        P("seq", "tensor"),
        P("seq"),
        P(),
        P("seq", "tensor"),
        P("seq", "tensor"),
        P("seq", "tensor"),
        P(),
        P(),
        P("tensor", "seq"),
        P("tensor"),
    )
    return jax.shard_map(
        body, mesh=mesh, in_specs=placed, out_specs=P("seq", "tensor"), check_vma=False
    )
```

time: 624 us -> 126 us (0.20); the launches traced: 615 us -> 125 us
  waiting for transfers between devices: 497 us -> 0 us
  Pallas kernels: 0 us -> 121 us
  blocking collectives: 39 us -> 0 us
  starting transfers between devices: 25.1 us -> 0 us
  matrix products: 17.4 us -> 0 us
  between operations: 13.7 us -> 0.01 us
  other arithmetic: 12 us -> 0.57 us
    all_gather x5 -> x0, waiting for transfers between devices: 411 us -> none  [the longest x1 94.5 us: body(): key_sum = accumulate(lax.all_gather(key_weight, 'seq', axis=0, tiled=True))]
    pallas_call x0 -> x1, Pallas kernels: none -> 121 us  [body(): pl.pallas_call(kernel, out_shape=jax.ShapeDtypeStruct((FEAT, TOK), BF16),...]
    reduce_scatter x1 -> x0, waiting for transfers between devices: 83.3 us -> none  [body(): lax.psum_scatter(term.astype(jnp.bfloat16), 'tensor', scatter_dimension=1...]
    psum x1 -> x0, blocking collectives: 39 us -> none  [body(): squares = lax.psum(jnp.sum(share * share, axis=-1), 'tensor')]
    ppermute x8 -> x0, starting transfers between devices: 24.9 us -> none  [passed_along(): lax.ppermute(value, axis, [(source, source + steps) for source in range(i...]
    dot_general x6 -> x0, matrix products: 17.4 us -> none  [the longest x3 10 us: accumulate(): return jnp.dot(normed, piece, preferred_element_type=jnp.float32)]
    unnamed x16 -> x3, local copies, waits for them, and re-layouts: 8.31 us -> 1.6 us
  transfers between devices with their start and end apart: 14 -> 0, of which waited for: 6 -> 0; matrix products, arithmetic and copies ran while one was open for 5% -> 0% of each run, Pallas kernels for 0% -> 0%
where the time goes in v1:
time: 126 us; the launch traced here: 125 us
  Pallas kernels  121 us (96%)
  local copies, waits for them, and re-layouts  3.91 us (3%)
    pallas_call x1, Pallas kernels, body(): pl.pallas_call(kernel, out_shape=jax.ShapeDtypeStruct((FEAT, TOK), BF16),...  121 us

profile of v1, /device:TPU:6, one launch (start us, length us, event | category | flops | bytes accessed | tf_op | source)
XLA Modules:
  0.0 125.2 jit_solution(6767931785643725633)
XLA Ops:
  0.0 0.8 dynamic_slice.3
  0.8 0.6 maximum_bitcast_fusion.inv_ref
  1.3 0.0 copy-start
  1.3 0.8 copy.11.gain_ref
  2.1 0.0 copy-done
  2.1 0.8 broadcast_in_dim.20.pg_ref
  2.9 120.7 %shard_map.100 = bf16[336,256]{1,0:T(8,128)(2,1)} custom-call(bf16[336,256]{1,0:T(8,128)(2,1)} %bitcast.11, s32[1,256]{1,0:T(1,128)} %bitcast.13, f32[168,1]{1,0:T(8,128)} %copy.11.gain_ref, bf16[168,256]{1,0:T(8,128)(2,1)} %wq_ref.1, bf16[168,128]{1,0:T(8,128)(2,1)} %wk_ref.1, bf16[168,128]{1,0:T(8,128)(2,1)} %wv_ref.1, f32[1,128]{1,0:T(1,128)} %bitcast.14, ...), custom_call_target="tpu_custom_call" | custom-call | flops 3000000000 | bytes 1000000 | tf_op jit(solution)/shard_map/pallas_call | solution.py:487
  123.6 1.6 %copy.14 = bf16[256,336]{0,1:T(8,128)(2,1)} copy(bf16[256,336]{0,1:T(8,128)(2,1)} %bitcast.9) | data formatting | bytes 344064
  (1 shorter events, 0.0 us)
Async XLA Ops:
  1.3 0.8 copy-start

commit v2 on v1

v2 whole, which is shorter than its diff:
```python
import jax
import jax.numpy as jnp
import numpy as np
from jax import lax
from jax.experimental import pallas as pl
from jax.experimental.pallas import tpu as pltpu
from jax.sharding import PartitionSpec as P

D = 5376
HEAD_DIM = 128
WINDOW = 1024
FEAT = 336
HALF = 168
TOK = 256
EPS = 1e-6
SCORE_SCALE = 168.0**-0.5
LOG2E = 1.4426950408889634
MESH = pl.DeviceIdType.MESH
F32 = jnp.float32
BF16 = jnp.bfloat16

REACH = ((4, 3), (3, 4))
KV, Q, OUT = 0, 1, 2
NT = (((1,), (1,)), ((), ()))


def kernel(
    h_ref,
    pos_ref,
    gain_ref,
    wq_ref,
    wk_ref,
    wv_ref,
    qg_ref,
    kg_ref,
    wo_ref,
    pg_ref,
    inv_ref,
    out_ref,
    xg,
    xt,
    wb,
    kv,
    qb,
    ctx,
    acc,
    sq,
    trig,
    oacc,
    zpart,
    xpart,
    zs,
    zr,
    xs,
    xr,
    rs,
    rr,
    ps,
    pr,
    bs,
    br,
    ms,
    mr,
    hs,
    hr,
    qs,
    qr,
    loc,
):
    s = lax.axis_index("seq")
    t = lax.axis_index("tensor")
    core = lax.rem(s, 2)
    c = s // 2
    y = lax.rem(c, 8)
    zh = c // 8
    x = t // 4
    zl = lax.rem(t, 4)
    other = 1 - core

    def at_seq(chip, which):
        return {"seq": chip * 2 + which, "tensor": t}

    def at_tensor(xx, zz):
        return {"seq": s, "tensor": lax.rem(xx + 8, 4) * 4 + zz}

    sibling = at_seq(c, other)
    far_half = at_seq((1 - zh) * 8 + y, core)
    y_up = at_seq(zh * 8 + lax.rem(y + 1, 8), core)
    y_down = at_seq(zh * 8 + lax.rem(y + 7, 8), core)
    next_chip = at_seq(lax.rem(c + 1, 16), core)
    prev_chip = at_seq(lax.rem(c + 15, 16), core)
    mirror = {"seq": t * 2 + core, "tensor": c}
    off_diagonal = c != t

    pending = []

    def send(src, dst, ssem, rsem, dev, cond=None):
        copy = pltpu.make_async_remote_copy(
            src_ref=src, dst_ref=dst, send_sem=ssem, recv_sem=rsem, device_id=dev, device_id_type=MESH
        )
        if cond is None:
            copy.start()
        else:
            pl.when(cond)(copy.start)
        pending.append((copy, cond))

    def recv(dst, ssem, rsem, cond=None):
        copy = pltpu.make_async_remote_copy(
            src_ref=dst, dst_ref=dst, send_sem=ssem, recv_sem=rsem, device_id=sibling, device_id_type=MESH
        )
        if cond is None:
            copy.wait_recv()
        else:
            pl.when(cond)(copy.wait_recv)

    barrier = pltpu.get_barrier_semaphore()
    peers = [sibling, far_half, y_up, y_down, next_chip, prev_chip]
    peers += [at_tensor(x + d, zl) for d in (1, 2, 3)]
    peers += [at_tensor(x, lax.rem(zl + d, 4)) for d in (1, 2, 3)]
    for peer in peers:
        pl.semaphore_signal(barrier, inc=1, device_id=peer, device_id_type=MESH)

    @pl.when(off_diagonal)
    def _():
        pl.semaphore_signal(barrier, inc=1, device_id=mirror, device_id_type=MESH)

    xg[t] = h_ref[...]
    first = s * HALF
    row0 = first // 128
    index = lax.broadcasted_iota(jnp.int32, (HALF, 128), 0) + (first - row0 * 128)
    lanes = lax.broadcasted_iota(jnp.int32, (HALF, 128), 1)
    gain = jnp.zeros((HALF, 128), F32)
    for i in range(3):
        line = gain_ref[pl.ds(jnp.minimum(row0 + i, D // 128 - 1), 1), :]
        gain = jnp.where(lanes + i * 128 == index, line, gain)
    gain = 1.0 + jnp.sum(gain, axis=1, keepdims=True)
    wb[KV, core, c, :, 0:128] = (wk_ref[...].astype(F32) * gain).astype(BF16)
    wb[KV, core, c, :, 128:256] = (wv_ref[...].astype(F32) * gain).astype(BF16)
    wb[Q, core, c] = (wq_ref[...].astype(F32) * gain).astype(BF16)

    pl.semaphore_wait(barrier, jnp.where(off_diagonal, len(peers) + 1, len(peers)))

    def near_z(n):
        if n == 0:
            return zl
        if n == 1:
            return zl + 1 - 2 * lax.rem(zl, 2)
        if n == 2:
            return 2 - zl // 2
        return 3 * (1 - zl // 2)

    class TensorFlow:
        def __init__(self, k, block):
            self.block = block
            self.k = k

        def slot(self, dx, n):
            return lax.rem(x + dx + 4, 4) * 4 + near_z(n)

        def to_x(self, n):
            blk = self.block(self.slot(0, n))
            for i, d in enumerate((1, 3, 2)):
                send(blk, blk, xs.at[self.k, n, i], xr.at[self.k, n, i], at_tensor(x + d, zl))

        def own(self):
            blk = self.block(t)
            send(blk, blk, zs.at[self.k, 0], zr.at[self.k, zl], at_tensor(x, lax.rem(zl + 1, 4)), zl < 3)
            send(blk, blk, zs.at[self.k, 4], zr.at[self.k, zl], at_tensor(x, lax.rem(zl + 3, 4)), zl > 0)
            self.to_x(0)

        def on_z(self, n):
            q = near_z(n)
            blk = self.block(self.slot(0, n))
            recv(blk, zs.at[self.k, n], zr.at[self.k, q])
            up = q < zl
            ok = jnp.where(up, zl < 3, zl > 0)
            dev = at_tensor(x, jnp.where(up, lax.rem(zl + 1, 4), lax.rem(zl + 3, 4)))
            send(blk, blk, zs.at[self.k, n], zr.at[self.k, q], dev, ok)
            self.to_x(n)

        def on_x(self, n, i):
            d = (1, 3, 2)[i]
            recv(self.block(self.slot(-d, n)), xs.at[self.k, n, i], xr.at[self.k, n, i])

    def w_slot(part, way, d):
        half = zh if part == 0 else 1 - zh
        yy = lax.rem(y + (8 - d if way == 0 else d), 8)
        return half * 8 + yy

    def ring_send(k, part, way, d):
        if d < REACH[part][way]:
            blk = wb.at[k, core, w_slot(part, way, d)]
            i = (part * 2 + way) * 4 + d
            send(blk, blk, rs.at[k, i], rr.at[k, i], y_up if way == 0 else y_down)

    def relay(k, j):
        blk = wb.at[k, core, j]
        send(blk, blk, bs.at[k, j], br.at[k, j], sibling)

    def on_rings(k, part, d):
        for way in (0, 1):
            if d <= REACH[part][way]:
                j = w_slot(part, way, d)
                i = (part * 2 + way) * 4 + d - 1
                recv(wb.at[k, core, j], rs.at[k, i], rr.at[k, i])
                ring_send(k, part, way, d)
                relay(k, j)

    def to_half(k):
        own = wb.at[k, core, c]
        send(own, own, ps.at[k], pr.at[k], far_half)

    def own_ring(k):
        for way in (0, 1):
            ring_send(k, 0, way, 0)

    def on_half(k):
        j = (1 - zh) * 8 + y
        recv(wb.at[k, core, j], ps.at[k], pr.at[k])
        for way in (0, 1):
            ring_send(k, 1, way, 0)
        relay(k, j)

    hidden = TensorFlow(0, lambda j: xg.at[j])
    own_ring(KV)
    to_half(KV)
    hidden.own()
    own_ring(Q)
    to_half(Q)
    relay(KV, c)
    relay(Q, c)

    pos_wide = jnp.transpose(jnp.broadcast_to(pos_ref[...].astype(F32), (HEAD_DIM, TOK)))
    angles = pos_wide * inv_ref[...]
    lane = lax.broadcasted_iota(jnp.int32, (TOK, HEAD_DIM), 1)
    trig[0] = jnp.cos(angles)
    sine = jnp.sin(angles)
    trig[1] = jnp.where(lane < HEAD_DIM // 2, -sine, sine)
    trig[2] = pos_wide

    sq[...] = jnp.zeros_like(sq)

    def take(j):
        block = xg[j].astype(F32)
        xt[j, 0] = jnp.transpose(block[0:HALF]).astype(BF16)
        xt[j, 1] = jnp.transpose(block[HALF:FEAT]).astype(BF16)
        sq[0:1, :] += jnp.sum(block * block, axis=0, keepdims=True)

    def take_x(n, i):
        hidden.on_x(n, i)
        take(hidden.slot(-(1, 3, 2)[i], n))

    def take_z(n):
        take(hidden.slot(0, n))

    on_rings(KV, 0, 1)
    hidden.on_z(1)
    on_rings(Q, 0, 1)
    on_half(KV)
    take(t)
    on_rings(KV, 0, 2)
    take_x(0, 0)
    take_x(0, 1)
    hidden.on_z(2)
    on_half(Q)
    on_rings(Q, 0, 2)
    on_rings(KV, 1, 1)

    send(wo_ref, wb.at[OUT, core, t], ms.at[0], mr.at[0], mirror, off_diagonal)

    @pl.when(jnp.logical_not(off_diagonal))
    def _():
        local = pltpu.make_async_copy(wo_ref, wb.at[OUT, core, c], loc)
        local.start()
        local.wait()

    take_z(1)
    on_rings(KV, 0, 3)
    take_x(0, 2)
    on_rings(Q, 1, 1)
    hidden.on_z(3)
    take_z(2)
    on_rings(Q, 0, 3)
    on_rings(KV, 1, 2)
    take_x(1, 0)
    take_x(1, 1)
    on_rings(KV, 0, 4)
    on_rings(Q, 1, 2)
    take_x(1, 2)
    on_rings(KV, 1, 3)
    on_rings(Q, 0, 4)
    take_x(2, 0)
    take_x(2, 1)
    on_rings(Q, 1, 3)
    on_rings(KV, 1, 4)
    recv(wb.at[OUT, core, c], ms.at[0], mr.at[0], off_diagonal)
    to_half(OUT)
    own_ring(OUT)
    relay(OUT, c)
    take_z(3)
    take_x(2, 2)
    on_rings(Q, 1, 4)
    take_x(3, 0)
    take_x(3, 1)
    take_x(3, 2)

    mean_sq = jnp.transpose(jnp.broadcast_to(sq[0:1, :], (HEAD_DIM, TOK))) / D

    def project(k):
        acc[...] = jnp.zeros_like(acc)

        def step(j, carry):
            recv(wb.at[k, other, j], bs.at[k, j], br.at[k, j])
            acc[...] += jnp.dot(xt[j, 0], wb[k, 0, j], preferred_element_type=F32) + jnp.dot(
                xt[j, 1], wb[k, 1, j], preferred_element_type=F32
            )
            return carry

        lax.fori_loop(0, 16, step, 0)

    def head(raw, gain_row):
        mean = jnp.mean(raw * raw, axis=-1, keepdims=True)
        unit = raw * lax.rsqrt(mean + EPS * (mean_sq + EPS)) * (1.0 + gain_row)
        return unit * trig[0] + pltpu.roll(unit, HEAD_DIM // 2, 1) * trig[1]

    project(KV)
    kv[4, 0] = head(acc[:, 0:128], kg_ref[...]).astype(BF16)
    kv[4, 1] = (acc[:, 128:256] * lax.rsqrt(mean_sq + EPS)).astype(BF16)

    send(kv.at[4], kv.at[2], hs.at[0], hr.at[2], next_chip, c < 15)
    send(kv.at[4], kv.at[3], hs.at[2], hr.at[3], sibling, core == 0)
    for i in range(4):

        @pl.when(s + i < 4)
        def _():
            kv[i] = jnp.zeros((2, TOK, HEAD_DIM), BF16)

    on_half(OUT)
    on_rings(OUT, 0, 1)
    project(Q)
    recv(kv.at[2], hs.at[0], hr.at[2], c >= 1)
    send(kv.at[2], kv.at[0], hs.at[1], hr.at[0], next_chip, jnp.logical_and(c >= 1, c < 15))
    send(kv.at[2], kv.at[1 + 2 * core], hs.at[3], hr.at[1 + 2 * core], sibling, c >= 1)
    for i in range(2):
        qb[i] = head(acc[:, i * 128 : (i + 1) * 128], qg_ref[...]).astype(BF16)
    on_rings(OUT, 0, 2)
    on_rings(OUT, 1, 1)
    recv(kv.at[0], hs.at[1], hr.at[0], c >= 2)
    send(kv.at[0], kv.at[1], hs.at[4], hr.at[1], sibling, jnp.logical_and(c >= 2, core == 1))
    recv(kv.at[3], hs.at[2], hr.at[3], s >= 1)
    on_rings(OUT, 0, 3)
    recv(kv.at[1], hs.at[3], hr.at[1], s >= 3)

    ROWS = 128

    def attend(hd, r):
        rows = pl.ds(pl.multiple_of(r * ROWS, ROWS), ROWS)
        query = qb[hd, rows, :]
        position = trig[2, rows, :].astype(jnp.int32)
        position = jnp.concatenate([position, position], axis=1)
        row = lax.broadcasted_iota(jnp.int32, (ROWS, TOK), 0) + r * ROWS
        col = lax.broadcasted_iota(jnp.int32, (ROWS, TOK), 1)
        limit = jnp.minimum(jnp.minimum(position, row + s * TOK), WINDOW - 1)
        scores = []
        for i in range(5):
            raw = lax.dot_general(query, kv[i, 0], NT, preferred_element_type=F32)
            gap = row + (4 - i) * TOK - col
            allowed = gap <= limit
            if i == 4:
                allowed = jnp.logical_and(allowed, gap >= 0)
            scores.append(jnp.where(allowed, raw, -1e30))
        peak = scores[0]
        for i in range(1, 5):
            peak = jnp.maximum(peak, scores[i])
        peak = jnp.max(peak, axis=-1, keepdims=True)
        total = jnp.zeros((ROWS, TOK), F32)
        mixed = jnp.zeros((ROWS, HEAD_DIM), F32)
        for i in range(5):
            expo = jnp.exp2((scores[i] - peak) * (SCORE_SCALE * LOG2E))
            total += expo
            mixed += jnp.dot(expo.astype(BF16), kv[i, 1], preferred_element_type=F32)
        mixed = mixed / jnp.sum(total, axis=-1, keepdims=True)
        ctx[hd, t, rows, :] = mixed.astype(BF16)

    contexts = []
    for hd in range(2):

        def rows_of(r, carry, hd=hd):
            attend(hd, r)
            return carry

        lax.fori_loop(0, 2, rows_of, 0)
        flow = TensorFlow(1 + hd, lambda j, hd=hd: ctx.at[hd, j])
        flow.own()
        contexts.append(flow)

    on_rings(OUT, 1, 2)
    on_rings(OUT, 0, 4)
    oacc[...] = jnp.zeros_like(oacc)

    def out_step(j):
        right = jnp.concatenate([ctx[0, j], ctx[1, j]], axis=1)
        for i in range(2):
            oacc[i] += lax.dot_general(wb[OUT, i, j], right, NT, preferred_element_type=F32)

    def c_z(n):
        for flow in contexts:
            flow.on_z(n)

    def c_x(n, i):
        for flow in contexts:
            flow.on_x(n, i)
        out_step(contexts[0].slot(-(1, 3, 2)[i], n))

    def out_z(n):
        out_step(contexts[0].slot(0, n))

    c_z(1)
    on_rings(OUT, 1, 3)
    c_z(2)
    on_rings(OUT, 1, 4)
    c_z(3)

    def wait_out(j, carry):
        recv(wb.at[OUT, other, j], bs.at[OUT, j], br.at[OUT, j])
        return carry

    lax.fori_loop(0, 16, wait_out, 0)
    out_step(t)
    for n in range(1, 4):
        out_z(n)
    for n in range(4):
        for i in range(3):
            c_x(n, i)

    def spread(buf, k, me, device):
        for i, d in enumerate((1, 2, 3)):
            send(buf.at[me], buf.at[me], qs.at[k, i], qr.at[k, me], device(lax.rem(me + d, 4)))
        for d in (1, 2, 3):
            j = lax.rem(me + d, 4)
            recv(buf.at[j], qs.at[k, d - 1], qr.at[k, j])
        return buf[0] + buf[1] + buf[2] + buf[3]

    squares = jnp.sum(oacc[0] * oacc[0] + oacc[1] * oacc[1], axis=0, keepdims=True)
    zpart[zl] = jnp.broadcast_to(squares, (8, TOK))
    xpart[x] = spread(zpart, 0, zl, lambda j: at_tensor(x, j))
    squares = spread(xpart, 1, x, lambda j: at_tensor(j, zl))
    scale = lax.rsqrt(squares[0:1, :] / D + EPS)
    diagonal = lax.broadcasted_iota(jnp.int32, (FEAT, FEAT), 0) == lax.broadcasted_iota(
        jnp.int32, (FEAT, FEAT), 1
    )
    post_gain = 1.0 + jnp.sum(jnp.where(diagonal, pg_ref[...][None, :], 0.0), axis=1, keepdims=True)
    attention = jnp.concatenate([oacc[0], oacc[1]], axis=0)
    out_ref[...] = (h_ref[...].astype(F32) + attention * scale * post_gain).astype(BF16)

    for copy, cond in pending:
        if cond is None:
            copy.wait_send()
        else:
            pl.when(cond)(copy.wait_send)


def body(
    hidden_in,
    positions,
    pre_gain,
    query_weight,
    key_weight,
    value_weight,
    query_gain,
    key_gain,
    output_weight,
    post_gain,
):
    exponent = np.arange(HEAD_DIM // 2, dtype=np.float32) * np.float32(2.0) / np.float32(HEAD_DIM)
    inverse = np.float32(1.0) / np.float32(10000.0) ** exponent
    inverse = np.concatenate([inverse, inverse])[None, :].astype(np.float32)
    vmem = pl.BlockSpec(memory_space=pltpu.VMEM)
    dma = pltpu.SemaphoreType.DMA
    out = pl.pallas_call(
        kernel,
        out_shape=jax.ShapeDtypeStruct((FEAT, TOK), BF16),
        in_specs=[vmem] * 11,
        out_specs=vmem,
        scratch_shapes=[
            pltpu.VMEM((16, FEAT, TOK), BF16),
            pltpu.VMEM((16, 2, TOK, HALF), BF16),
            pltpu.VMEM((3, 2, 16, HALF, 256), BF16),
            pltpu.VMEM((5, 2, TOK, HEAD_DIM), BF16),
            pltpu.VMEM((2, TOK, HEAD_DIM), BF16),
            pltpu.VMEM((2, 16, TOK, HEAD_DIM), BF16),
            pltpu.VMEM((TOK, 256), F32),
            pltpu.VMEM((8, TOK), F32),
            pltpu.VMEM((3, TOK, HEAD_DIM), F32),
            pltpu.VMEM((2, HALF, TOK), F32),
            pltpu.VMEM((4, 8, TOK), F32),
            pltpu.VMEM((4, 8, TOK), F32),
            dma((3, 5)),
            dma((3, 4)),
            dma((3, 4, 3)),
            dma((3, 4, 3)),
            dma((3, 16)),
            dma((3, 16)),
            dma((3,)),
            dma((3,)),
            dma((3, 16)),
            dma((3, 16)),
            dma((1,)),
            dma((1,)),
            dma((5,)),
            dma((5,)),
            dma((2, 3)),
            dma((2, 4)),
            dma,
        ],
        compiler_params=pltpu.CompilerParams(
            collective_id=0, has_side_effects=True, vmem_limit_bytes=56 << 20
        ),
        cost_estimate=pl.CostEstimate(flops=3_000_000_000, bytes_accessed=1_000_000, transcendentals=1_000_000),
    )(
        hidden_in.T,
        positions[None, :],
        pre_gain.reshape(D // 128, 128),
        query_weight,
        key_weight,
        value_weight,
        query_gain[None, :],
        key_gain[None, :],
        output_weight.T,
        post_gain,
        inverse,
    )
    return out.T


def solution(mesh):
    placed = (
        P("seq", "tensor"),
        P("seq"),
        P(),
        P("seq", "tensor"),
        P("seq", "tensor"),
        P("seq", "tensor"),
        P(),
        P(),
        P("tensor", "seq"),
        P("tensor"),
    )
    return jax.shard_map(
        body, mesh=mesh, in_specs=placed, out_specs=P("seq", "tensor"), check_vma=False
    )
```

time: 126 us -> 110 us (0.87)
  Pallas kernels: 121 us -> 108 us
  local copies, waits for them, and re-layouts: 3.91 us -> 1.6 us
    pallas_call x1, Pallas kernels: 121 us -> 108 us  [body(): pl.pallas_call(kernel, out_shape=jax.ShapeDtypeStruct((FEAT, TOK), BF16),...]
where the time goes in v2:
time: 110 us
  Pallas kernels  108 us (98%)
  local copies, waits for them, and re-layouts  1.6 us (1%)
    pallas_call x1, Pallas kernels, body(): pl.pallas_call(kernel, out_shape=jax.ShapeDtypeStruct((FEAT, TOK), BF16),...  108 us

profile of v2, /device:TPU:6, one launch (start us, length us, event | category | flops | bytes accessed | tf_op | source)
XLA Modules:
  0.0 110.0 jit_solution(13616068296879719495)
XLA Ops:
  0.0 108.4 %shard_map.109 = bf16[336,256]{1,0:T(8,128)(2,1)} custom-call(bf16[336,256]{1,0:T(8,128)(2,1)} %bitcast.8, s32[1,256]{1,0:T(1,128)} %bitcast.11, f32[42,128]{1,0:T(8,128)} %bitcast.10, bf16[168,256]{1,0:T(8,128)(2,1)} %wq_ref.1, bf16[168,128]{1,0:T(8,128)(2,1)} %wk_ref.1, bf16[168,128]{1,0:T(8,128)(2,1)} %wv_ref.1, f32[1,128]{1,0:T(1,128)} %bitcast.12, ...), custom_call_target="tpu_custom_call" | custom-call | flops 3000000000 | bytes 1000000 | tf_op jit(solution)/shard_map/pallas_call | solution.py:480
  108.4 1.6 %copy.13 = bf16[256,336]{0,1:T(8,128)(2,1)} copy(bf16[256,336]{0,1:T(8,128)(2,1)} %bitcast.7) | data formatting | bytes 344064

commit v3 on v2

--- a/solution.py
+++ b/solution.py
@@ -89,8 +89,10 @@
     y_down = at_seq(zh * 8 + lax.rem(y + 7, 8), core)
     next_chip = at_seq(lax.rem(c + 1, 16), core)
     prev_chip = at_seq(lax.rem(c + 15, 16), core)
-    mirror = {"seq": t * 2 + core, "tensor": c}
-    off_diagonal = c != t
+    out_home = lax.rem(t, 2) * 8 + lax.rem(y + t // 2, 8)
+    out_to = {"seq": out_home * 2 + core, "tensor": c}
+    out_from = {"seq": t * 2 + core, "tensor": lax.rem(y + 8 - lax.rem(t, 8), 8) * 2 + zh}
+    moves = jnp.logical_or(c != t, out_home != c)
 
     pending = []
 
@@ -120,11 +122,13 @@
     for peer in peers:
         pl.semaphore_signal(barrier, inc=1, device_id=peer, device_id_type=MESH)
 
-    @pl.when(off_diagonal)
+    @pl.when(moves)
     def _():
-        pl.semaphore_signal(barrier, inc=1, device_id=mirror, device_id_type=MESH)
-
-    xg[t] = h_ref[...]
+        for peer in (out_to, out_from):
+            pl.semaphore_signal(barrier, inc=1, device_id=peer, device_id_type=MESH)
+
+    xg[0, t] = h_ref[:, 0:128]
+    xg[1, t] = h_ref[:, 128:256]
     first = s * HALF
     row0 = first // 128
     index = lax.broadcasted_iota(jnp.int32, (HALF, 128), 0) + (first - row0 * 128)
@@ -138,7 +142,7 @@
     wb[KV, core, c, :, 128:256] = (wv_ref[...].astype(F32) * gain).astype(BF16)
     wb[Q, core, c] = (wq_ref[...].astype(F32) * gain).astype(BF16)
 
-    pl.semaphore_wait(barrier, jnp.where(off_diagonal, len(peers) + 1, len(peers)))
+    pl.semaphore_wait(barrier, jnp.where(moves, len(peers) + 2, len(peers)))
 
     def near_z(n):
         if n == 0:
@@ -157,16 +161,18 @@
         def slot(self, dx, n):
             return lax.rem(x + dx + 4, 4) * 4 + near_z(n)
 
+        def way(self, n):
+            return lax.rem(core + n, 2)
+
         def to_x(self, n):
             blk = self.block(self.slot(0, n))
-            for i, d in enumerate((1, 3, 2)):
+            for i, d in enumerate((1, 3)):
                 send(blk, blk, xs.at[self.k, n, i], xr.at[self.k, n, i], at_tensor(x + d, zl))
 
-        def own(self):
+        def own_z(self):
             blk = self.block(t)
             send(blk, blk, zs.at[self.k, 0], zr.at[self.k, zl], at_tensor(x, lax.rem(zl + 1, 4)), zl < 3)
             send(blk, blk, zs.at[self.k, 4], zr.at[self.k, zl], at_tensor(x, lax.rem(zl + 3, 4)), zl > 0)
-            self.to_x(0)
 
         def on_z(self, n):
             q = near_z(n)
@@ -178,9 +184,24 @@
             send(blk, blk, zs.at[self.k, n], zr.at[self.k, q], dev, ok)
             self.to_x(n)
 
-        def on_x(self, n, i):
-            d = (1, 3, 2)[i]
-            recv(self.block(self.slot(-d, n)), xs.at[self.k, n, i], xr.at[self.k, n, i])
+        def relay_x(self, n):
+            i = self.way(n)
+            d = 1 - 2 * i
+            j = self.slot(-d, n)
+            recv(self.block(j), xs.at[self.k, n, 0], xr.at[self.k, n, i])
+            send(self.block(j), self.block(j), xs.at[self.k, n, 2], xr.at[self.k, n, 2], at_tensor(x + d, zl))
+            return j
+
+        def near(self, n):
+            i = 1 - self.way(n)
+            j = self.slot(2 * i - 1, n)
+            recv(self.block(j), xs.at[self.k, n, 0], xr.at[self.k, n, i])
+            return j
+
+        def far(self, n):
+            j = self.slot(2, n)
+            recv(self.block(j), xs.at[self.k, n, 2], xr.at[self.k, n, 2])
+            return j
 
     def w_slot(part, way, d):
         half = zh if part == 0 else 1 - zh
@@ -197,14 +218,17 @@
         blk = wb.at[k, core, j]
         send(blk, blk, bs.at[k, j], br.at[k, j], sibling)
 
+    def on_ring(k, part, d, way):
+        j = w_slot(part, way, d)
+        i = (part * 2 + way) * 4 + d - 1
+        recv(wb.at[k, core, j], rs.at[k, i], rr.at[k, i])
+        ring_send(k, part, way, d)
+        relay(k, j)
+
     def on_rings(k, part, d):
         for way in (0, 1):
             if d <= REACH[part][way]:
-                j = w_slot(part, way, d)
-                i = (part * 2 + way) * 4 + d - 1
-                recv(wb.at[k, core, j], rs.at[k, i], rr.at[k, i])
-                ring_send(k, part, way, d)
-                relay(k, j)
+                on_ring(k, part, d, way)
 
     def to_half(k):
         own = wb.at[k, core, c]
@@ -221,10 +245,13 @@
             ring_send(k, 1, way, 0)
         relay(k, j)
 
-    hidden = TensorFlow(0, lambda j: xg.at[j])
+    halves = [TensorFlow(k, lambda j, k=k: xg.at[k, j]) for k in range(2)]
     own_ring(KV)
     to_half(KV)
-    hidden.own()
+    halves[0].own_z()
+    halves[0].to_x(0)
+    halves[1].own_z()
+    halves[1].to_x(0)
     own_ring(Q)
     to_half(Q)
     relay(KV, c)
@@ -240,69 +267,101 @@
 
     sq[...] = jnp.zeros_like(sq)
 
-    def take(j):
-        block = xg[j].astype(F32)
-        xt[j, 0] = jnp.transpose(block[0:HALF]).astype(BF16)
-        xt[j, 1] = jnp.transpose(block[HALF:FEAT]).astype(BF16)
-        sq[0:1, :] += jnp.sum(block * block, axis=0, keepdims=True)
-
-    def take_x(n, i):
-        hidden.on_x(n, i)
-        take(hidden.slot(-(1, 3, 2)[i], n))
-
-    def take_z(n):
-        take(hidden.slot(0, n))
-
-    on_rings(KV, 0, 1)
-    hidden.on_z(1)
-    on_rings(Q, 0, 1)
+    def take(k, j):
+        block = xg[k, j].astype(F32)
+        tokens = slice(k * 128, (k + 1) * 128)
+        xt[j, 0, tokens] = jnp.transpose(block[0:HALF]).astype(BF16)
+        xt[j, 1, tokens] = jnp.transpose(block[HALF:FEAT]).astype(BF16)
+        sq[0:1, tokens] += jnp.sum(block * block, axis=0, keepdims=True)
+
+    def on_z(n, k):
+        halves[k].on_z(n)
+
+    def relay_x(n, k):
+        take(k, halves[k].relay_x(n))
+
+    def near(n, k):
+        take(k, halves[k].near(n))
+
+    def far(n, k):
+        take(k, halves[k].far(n))
+
+    take(0, t)
+    take(1, t)
+    on_ring(KV, 0, 1, 0)
+    on_ring(KV, 0, 1, 1)
+    relay_x(0, 0)
+    on_z(1, 0)
+    near(0, 0)
+    on_ring(Q, 0, 1, 0)
+    on_ring(Q, 0, 1, 1)
+    relay_x(0, 1)
+    near(0, 1)
+    far(0, 0)
+    on_ring(KV, 0, 2, 0)
+    on_ring(KV, 0, 2, 1)
     on_half(KV)
-    take(t)
-    on_rings(KV, 0, 2)
-    take_x(0, 0)
-    take_x(0, 1)
-    hidden.on_z(2)
+    take(0, halves[0].slot(0, 1))
+    on_z(1, 1)
+    relay_x(1, 0)
+    on_ring(Q, 0, 2, 0)
+    on_ring(Q, 0, 2, 1)
+    on_z(2, 0)
+    near(1, 0)
+    far(0, 1)
     on_half(Q)
-    on_rings(Q, 0, 2)
-    on_rings(KV, 1, 1)
-
-    send(wo_ref, wb.at[OUT, core, t], ms.at[0], mr.at[0], mirror, off_diagonal)
-
-    @pl.when(jnp.logical_not(off_diagonal))
+    take(1, halves[1].slot(0, 1))
+    on_ring(KV, 0, 3, 0)
+    on_ring(KV, 0, 3, 1)
+    relay_x(1, 1)
+    on_z(2, 1)
+    send(wo_ref, wb.at[OUT, core, out_home], ms.at[0], mr.at[0], out_to, moves)
+
+    @pl.when(jnp.logical_not(moves))
     def _():
         local = pltpu.make_async_copy(wo_ref, wb.at[OUT, core, c], loc)
         local.start()
         local.wait()
-
-    take_z(1)
-    on_rings(KV, 0, 3)
-    take_x(0, 2)
-    on_rings(Q, 1, 1)
-    hidden.on_z(3)
-    take_z(2)
-    on_rings(Q, 0, 3)
-    on_rings(KV, 1, 2)
-    take_x(1, 0)
-    take_x(1, 1)
-    on_rings(KV, 0, 4)
-    on_rings(Q, 1, 2)
-    take_x(1, 2)
-    on_rings(KV, 1, 3)
-    on_rings(Q, 0, 4)
-    take_x(2, 0)
-    take_x(2, 1)
-    on_rings(Q, 1, 3)
-    on_rings(KV, 1, 4)
-    recv(wb.at[OUT, core, c], ms.at[0], mr.at[0], off_diagonal)
+    take(0, halves[0].slot(0, 2))
+    on_ring(KV, 1, 1, 0)
+    on_ring(KV, 1, 1, 1)
+    near(1, 1)
+    far(1, 0)
+    relay_x(2, 0)
+    take(1, halves[1].slot(0, 2))
+    on_z(3, 0)
+    on_ring(Q, 0, 3, 0)
+    on_ring(Q, 0, 3, 1)
+    near(2, 0)
+    far(1, 1)
+    on_ring(Q, 1, 1, 0)
+    on_ring(Q, 1, 1, 1)
+    relay_x(2, 1)
+    take(0, halves[0].slot(0, 3))
+    on_z(3, 1)
+    on_ring(KV, 0, 4, 0)
+    on_ring(KV, 1, 2, 1)
+    near(2, 1)
+    far(2, 0)
+    relay_x(3, 0)
+    on_ring(KV, 1, 2, 0)
+    on_ring(Q, 1, 2, 1)
+    take(1, halves[1].slot(0, 3))
+    near(3, 0)
+    far(2, 1)
+    on_ring(KV, 1, 3, 1)
+    on_ring(Q, 0, 4, 0)
+    relay_x(3, 1)
+    on_ring(Q, 1, 2, 0)
+    on_ring(Q, 1, 3, 1)
+    recv(wb.at[OUT, core, c], ms.at[0], mr.at[0], moves)
     to_half(OUT)
-    own_ring(OUT)
     relay(OUT, c)
-    take_z(3)
-    take_x(2, 2)
-    on_rings(Q, 1, 4)
-    take_x(3, 0)
-    take_x(3, 1)
-    take_x(3, 2)
+    near(3, 1)
+    far(3, 0)
+    on_ring(KV, 1, 3, 0)
+    on_ring(KV, 1, 4, 1)
+    far(3, 1)
 
     mean_sq = jnp.transpose(jnp.broadcast_to(sq[0:1, :], (HEAD_DIM, TOK))) / D
 
@@ -327,29 +386,32 @@
     kv[4, 0] = head(acc[:, 0:128], kg_ref[...]).astype(BF16)
     kv[4, 1] = (acc[:, 128:256] * lax.rsqrt(mean_sq + EPS)).astype(BF16)
 
-    send(kv.at[4], kv.at[2], hs.at[0], hr.at[2], next_chip, c < 15)
-    send(kv.at[4], kv.at[3], hs.at[2], hr.at[3], sibling, core == 0)
+    for v in range(2):
+        send(kv.at[4, v], kv.at[2, v], hs.at[0, v], hr.at[2, v], next_chip, c < 15)
+        send(kv.at[4, v], kv.at[3, v], hs.at[2, v], hr.at[3, v], sibling, core == 0)
     for i in range(4):
 
         @pl.when(s + i < 4)
         def _():
             kv[i] = jnp.zeros((2, TOK, HEAD_DIM), BF16)
 
-    on_half(OUT)
-    on_rings(OUT, 0, 1)
+    on_ring(Q, 1, 3, 0)
+    on_ring(Q, 1, 4, 1)
     project(Q)
-    recv(kv.at[2], hs.at[0], hr.at[2], c >= 1)
-    send(kv.at[2], kv.at[0], hs.at[1], hr.at[0], next_chip, jnp.logical_and(c >= 1, c < 15))
-    send(kv.at[2], kv.at[1 + 2 * core], hs.at[3], hr.at[1 + 2 * core], sibling, c >= 1)
     for i in range(2):
         qb[i] = head(acc[:, i * 128 : (i + 1) * 128], qg_ref[...]).astype(BF16)
-    on_rings(OUT, 0, 2)
-    on_rings(OUT, 1, 1)
-    recv(kv.at[0], hs.at[1], hr.at[0], c >= 2)
-    send(kv.at[0], kv.at[1], hs.at[4], hr.at[1], sibling, jnp.logical_and(c >= 2, core == 1))
-    recv(kv.at[3], hs.at[2], hr.at[3], s >= 1)
-    on_rings(OUT, 0, 3)
-    recv(kv.at[1], hs.at[3], hr.at[1], s >= 3)
+    for v in range(2):
+        recv(kv.at[2, v], hs.at[0, v], hr.at[2, v], c >= 1)
+        send(kv.at[2, v], kv.at[0, v], hs.at[1, v], hr.at[0, v], next_chip, jnp.logical_and(c >= 1, c < 15))
+        send(kv.at[2, v], kv.at[1 + 2 * core, v], hs.at[3, v], hr.at[1 + 2 * core, v], sibling, c >= 1)
+    for v in range(2):
+        recv(kv.at[0, v], hs.at[1, v], hr.at[0, v], c >= 2)
+        send(kv.at[0, v], kv.at[1, v], hs.at[4, v], hr.at[1, v], sibling, jnp.logical_and(c >= 2, core == 1))
+    own_ring(OUT)
+    on_half(OUT)
+    for v in range(2):
+        recv(kv.at[3, v], hs.at[2, v], hr.at[3, v], s >= 1)
+        recv(kv.at[1, v], hs.at[3, v], hr.at[1, v], s >= 3)
 
     ROWS = 128
 
@@ -390,36 +452,51 @@
             return carry
 
         lax.fori_loop(0, 2, rows_of, 0)
-        flow = TensorFlow(1 + hd, lambda j, hd=hd: ctx.at[hd, j])
-        flow.own()
+        flow = TensorFlow(2 + hd, lambda j, hd=hd: ctx.at[hd, j])
+        flow.own_z()
+        flow.to_x(0)
         contexts.append(flow)
 
-    on_rings(OUT, 1, 2)
-    on_rings(OUT, 0, 4)
     oacc[...] = jnp.zeros_like(oacc)
 
     def out_step(j):
         right = jnp.concatenate([ctx[0, j], ctx[1, j]], axis=1)
+        place = lax.rem(j, 2) * 8 + lax.rem(t + j // 2, 8)
         for i in range(2):
-            oacc[i] += lax.dot_general(wb[OUT, i, j], right, NT, preferred_element_type=F32)
-
-    def c_z(n):
-        for flow in contexts:
-            flow.on_z(n)
-
-    def c_x(n, i):
-        for flow in contexts:
-            flow.on_x(n, i)
-        out_step(contexts[0].slot(-(1, 3, 2)[i], n))
-
-    def out_z(n):
-        out_step(contexts[0].slot(0, n))
-
-    c_z(1)
+            oacc[i] += lax.dot_general(wb[OUT, i, place], right, NT, preferred_element_type=F32)
+
+    on_rings(OUT, 0, 1)
+    on_rings(OUT, 1, 1)
+    contexts[0].relay_x(0)
+    contexts[0].on_z(1)
+    contexts[1].relay_x(0)
+    contexts[1].on_z(1)
+    on_rings(OUT, 0, 2)
+    on_rings(OUT, 1, 2)
+    contexts[0].on_z(2)
+    contexts[0].relay_x(1)
+    contexts[1].on_z(2)
+    contexts[1].relay_x(1)
+    on_rings(OUT, 0, 3)
     on_rings(OUT, 1, 3)
-    c_z(2)
+    contexts[0].on_z(3)
+    contexts[0].relay_x(2)
+    contexts[1].on_z(3)
+    contexts[1].relay_x(2)
+    on_rings(OUT, 0, 4)
     on_rings(OUT, 1, 4)
-    c_z(3)
+    contexts[0].relay_x(3)
+    contexts[1].relay_x(3)
+
+    def drain():
+        for copy, cond in pending:
+            if cond is None:
+                copy.wait_send()
+            else:
+                pl.when(cond)(copy.wait_send)
+        pending.clear()
+
+    drain()
 
     def wait_out(j, carry):
         recv(wb.at[OUT, other, j], bs.at[OUT, j], br.at[OUT, j])
@@ -428,10 +505,16 @@
     lax.fori_loop(0, 16, wait_out, 0)
     out_step(t)
     for n in range(1, 4):
-        out_z(n)
+        out_step(contexts[0].slot(0, n))
     for n in range(4):
-        for i in range(3):
-            c_x(n, i)
+        out_step(contexts[0].slot(2 * contexts[0].way(n) - 1, n))
+    for n in range(4):
+        for flow in contexts:
+            near = flow.near(n)
+        out_step(near)
+        for flow in contexts:
+            far = flow.far(n)
+        out_step(far)
 
     def spread(buf, k, me, device):
         for i, d in enumerate((1, 2, 3)):
@@ -453,11 +536,7 @@
     attention = jnp.concatenate([oacc[0], oacc[1]], axis=0)
     out_ref[...] = (h_ref[...].astype(F32) + attention * scale * post_gain).astype(BF16)
 
-    for copy, cond in pending:
-        if cond is None:
-            copy.wait_send()
-        else:
-            pl.when(cond)(copy.wait_send)
+    drain()
 
 
 def body(
@@ -483,7 +562,7 @@
         in_specs=[vmem] * 11,
         out_specs=vmem,
         scratch_shapes=[
-            pltpu.VMEM((16, FEAT, TOK), BF16),
+            pltpu.VMEM((2, 16, FEAT, 128), BF16),
             pltpu.VMEM((16, 2, TOK, HALF), BF16),
             pltpu.VMEM((3, 2, 16, HALF, 256), BF16),
             pltpu.VMEM((5, 2, TOK, HEAD_DIM), BF16),
@@ -495,10 +574,10 @@
             pltpu.VMEM((2, HALF, TOK), F32),
             pltpu.VMEM((4, 8, TOK), F32),
             pltpu.VMEM((4, 8, TOK), F32),
-            dma((3, 5)),
-            dma((3, 4)),
-            dma((3, 4, 3)),
-            dma((3, 4, 3)),
+            dma((4, 5)),
+            dma((4, 4)),
+            dma((4, 4, 3)),
+            dma((4, 4, 3)),
             dma((3, 16)),
             dma((3, 16)),
             dma((3,)),
@@ -507,8 +586,8 @@
             dma((3, 16)),
             dma((1,)),
             dma((1,)),
-            dma((5,)),
-            dma((5,)),
+            dma((5, 2)),
+            dma((5, 2)),
             dma((2, 3)),
             dma((2, 4)),
             dma,

time: 110 us -> 103 us (0.936)
  Pallas kernels: 108 us -> 101 us
    pallas_call x1, Pallas kernels: 108 us -> 101 us  [body(): pl.pallas_call(kernel, out_shape=jax.ShapeDtypeStruct((FEAT, TOK), BF16),...]
where the time goes in v3:
time: 103 us
  Pallas kernels  101 us (98%)
  local copies, waits for them, and re-layouts  1.6 us (2%)
    pallas_call x1, Pallas kernels, body(): pl.pallas_call(kernel, out_shape=jax.ShapeDtypeStruct((FEAT, TOK), BF16),...  101 us

profile of v3, /device:TPU:6, one launch (start us, length us, event | category | flops | bytes accessed | tf_op | source)
XLA Modules:
  0.0 102.6 jit_solution(965229435798468598)
XLA Ops:
  0.0 101.0 %shard_map.109 = bf16[336,256]{1,0:T(8,128)(2,1)} custom-call(bf16[336,256]{1,0:T(8,128)(2,1)} %bitcast.8, s32[1,256]{1,0:T(1,128)} %bitcast.11, f32[42,128]{1,0:T(8,128)} %bitcast.10, bf16[168,256]{1,0:T(8,128)(2,1)} %wq_ref.1, bf16[168,128]{1,0:T(8,128)(2,1)} %wk_ref.1, bf16[168,128]{1,0:T(8,128)(2,1)} %wv_ref.1, f32[1,128]{1,0:T(1,128)} %bitcast.12, ...), custom_call_target="tpu_custom_call" | custom-call | flops 3000000000 | bytes 1000000 | tf_op jit(solution)/shard_map/pallas_call | solution.py:559
  101.0 1.6 %copy.13 = bf16[256,336]{0,1:T(8,128)(2,1)} copy(bf16[256,336]{0,1:T(8,128)(2,1)} %bitcast.7) | data formatting | bytes 344064

commit v4 on v3

--- a/solution.py
+++ b/solution.py
@@ -25,18 +25,24 @@
 
 
 def kernel(
-    h_ref,
+    h_in,
     pos_ref,
     gain_ref,
+    wq_in,
+    wk_in,
+    wv_in,
+    qg_ref,
+    kg_ref,
+    wo_in,
+    pg_ref,
+    inv_ref,
+    out_ref,
+    h_ref,
     wq_ref,
     wk_ref,
     wv_ref,
-    qg_ref,
-    kg_ref,
     wo_ref,
-    pg_ref,
-    inv_ref,
-    out_ref,
+    ld,
     xg,
     xt,
     wb,
@@ -127,8 +133,11 @@
         for peer in (out_to, out_from):
             pl.semaphore_signal(barrier, inc=1, device_id=peer, device_id_type=MESH)
 
-    xg[0, t] = h_ref[:, 0:128]
-    xg[1, t] = h_ref[:, 128:256]
+    pairs = ((wk_in, wk_ref), (wv_in, wv_ref), (h_in, h_ref), (wq_in, wq_ref), (wo_in, wo_ref))
+    loads = [pltpu.make_async_copy(src, dst, ld.at[i]) for i, (src, dst) in enumerate(pairs)]
+    for copy in loads:
+        copy.start()
+
     first = s * HALF
     row0 = first // 128
     index = lax.broadcasted_iota(jnp.int32, (HALF, 128), 0) + (first - row0 * 128)
@@ -138,10 +147,14 @@
         line = gain_ref[pl.ds(jnp.minimum(row0 + i, D // 128 - 1), 1), :]
         gain = jnp.where(lanes + i * 128 == index, line, gain)
     gain = 1.0 + jnp.sum(gain, axis=1, keepdims=True)
+    for copy in loads:
+        copy.wait()
     wb[KV, core, c, :, 0:128] = (wk_ref[...].astype(F32) * gain).astype(BF16)
     wb[KV, core, c, :, 128:256] = (wv_ref[...].astype(F32) * gain).astype(BF16)
     wb[Q, core, c] = (wq_ref[...].astype(F32) * gain).astype(BF16)
 
+    xg[0, t] = h_ref[:, 0:128]
+    xg[1, t] = h_ref[:, 128:256]
     pl.semaphore_wait(barrier, jnp.where(moves, len(peers) + 2, len(peers)))
 
     def near_z(n):
@@ -252,8 +265,6 @@
     halves[0].to_x(0)
     halves[1].own_z()
     halves[1].to_x(0)
-    own_ring(Q)
-    to_half(Q)
     relay(KV, c)
     relay(Q, c)
 
@@ -291,30 +302,8 @@
     on_ring(KV, 0, 1, 0)
     on_ring(KV, 0, 1, 1)
     relay_x(0, 0)
-    on_z(1, 0)
-    near(0, 0)
-    on_ring(Q, 0, 1, 0)
-    on_ring(Q, 0, 1, 1)
-    relay_x(0, 1)
-    near(0, 1)
-    far(0, 0)
-    on_ring(KV, 0, 2, 0)
-    on_ring(KV, 0, 2, 1)
-    on_half(KV)
-    take(0, halves[0].slot(0, 1))
-    on_z(1, 1)
-    relay_x(1, 0)
-    on_ring(Q, 0, 2, 0)
-    on_ring(Q, 0, 2, 1)
-    on_z(2, 0)
-    near(1, 0)
-    far(0, 1)
-    on_half(Q)
-    take(1, halves[1].slot(0, 1))
-    on_ring(KV, 0, 3, 0)
-    on_ring(KV, 0, 3, 1)
-    relay_x(1, 1)
-    on_z(2, 1)
+    own_ring(Q)
+    to_half(Q)
     send(wo_ref, wb.at[OUT, core, out_home], ms.at[0], mr.at[0], out_to, moves)
 
     @pl.when(jnp.logical_not(moves))
@@ -322,47 +311,70 @@
         local = pltpu.make_async_copy(wo_ref, wb.at[OUT, core, c], loc)
         local.start()
         local.wait()
-    take(0, halves[0].slot(0, 2))
+    on_z(1, 0)
+    near(0, 0)
+    relay_x(0, 1)
+    on_ring(KV, 0, 2, 0)
+    on_ring(KV, 0, 2, 1)
+    on_half(KV)
+    near(0, 1)
+    far(0, 0)
+    take(0, halves[0].slot(0, 1))
+    on_z(1, 1)
+    relay_x(1, 0)
+    on_ring(Q, 0, 1, 0)
+    on_ring(Q, 0, 1, 1)
+    on_z(2, 0)
+    near(1, 0)
+    far(0, 1)
+    on_ring(KV, 0, 3, 0)
+    on_ring(KV, 0, 3, 1)
+    on_half(Q)
+    take(1, halves[1].slot(0, 1))
+    relay_x(1, 1)
+    on_z(2, 1)
     on_ring(KV, 1, 1, 0)
     on_ring(KV, 1, 1, 1)
+    take(0, halves[0].slot(0, 2))
     near(1, 1)
     far(1, 0)
+    on_ring(Q, 0, 2, 0)
+    on_ring(Q, 0, 2, 1)
     relay_x(2, 0)
     take(1, halves[1].slot(0, 2))
     on_z(3, 0)
-    on_ring(Q, 0, 3, 0)
-    on_ring(Q, 0, 3, 1)
     near(2, 0)
     far(1, 1)
-    on_ring(Q, 1, 1, 0)
+    on_ring(KV, 0, 4, 0)
     on_ring(Q, 1, 1, 1)
     relay_x(2, 1)
     take(0, halves[0].slot(0, 3))
     on_z(3, 1)
-    on_ring(KV, 0, 4, 0)
     on_ring(KV, 1, 2, 1)
+    on_ring(Q, 1, 1, 0)
     near(2, 1)
     far(2, 0)
+    on_ring(KV, 1, 2, 0)
+    on_ring(Q, 0, 3, 1)
     relay_x(3, 0)
-    on_ring(KV, 1, 2, 0)
+    take(1, halves[1].slot(0, 3))
+    recv(wb.at[OUT, core, c], ms.at[0], mr.at[0], moves)
+    relay(OUT, c)
+    to_half(OUT)
+    near(3, 0)
+    on_ring(Q, 0, 3, 0)
     on_ring(Q, 1, 2, 1)
-    take(1, halves[1].slot(0, 3))
-    near(3, 0)
     far(2, 1)
+    relay_x(3, 1)
     on_ring(KV, 1, 3, 1)
-    on_ring(Q, 0, 4, 0)
-    relay_x(3, 1)
     on_ring(Q, 1, 2, 0)
-    on_ring(Q, 1, 3, 1)
-    recv(wb.at[OUT, core, c], ms.at[0], mr.at[0], moves)
-    to_half(OUT)
-    relay(OUT, c)
     near(3, 1)
     far(3, 0)
     on_ring(KV, 1, 3, 0)
+    on_ring(Q, 1, 3, 1)
+    far(3, 1)
     on_ring(KV, 1, 4, 1)
-    far(3, 1)
-
+    on_ring(Q, 0, 4, 0)
     mean_sq = jnp.transpose(jnp.broadcast_to(sq[0:1, :], (HEAD_DIM, TOK))) / D
 
     def project(k):
@@ -400,13 +412,16 @@
     project(Q)
     for i in range(2):
         qb[i] = head(acc[:, i * 128 : (i + 1) * 128], qg_ref[...]).astype(BF16)
-    for v in range(2):
-        recv(kv.at[2, v], hs.at[0, v], hr.at[2, v], c >= 1)
-        send(kv.at[2, v], kv.at[0, v], hs.at[1, v], hr.at[0, v], next_chip, jnp.logical_and(c >= 1, c < 15))
-        send(kv.at[2, v], kv.at[1 + 2 * core, v], hs.at[3, v], hr.at[1 + 2 * core, v], sibling, c >= 1)
-    for v in range(2):
-        recv(kv.at[0, v], hs.at[1, v], hr.at[0, v], c >= 2)
-        send(kv.at[0, v], kv.at[1, v], hs.at[4, v], hr.at[1, v], sibling, jnp.logical_and(c >= 2, core == 1))
+    recv(kv.at[2, 0], hs.at[0, 0], hr.at[2, 0], c >= 1)
+    send(kv.at[2, 0], kv.at[0, 0], hs.at[1, 0], hr.at[0, 0], next_chip, jnp.logical_and(c >= 1, c < 15))
+    send(kv.at[2, 0], kv.at[1 + 2 * core, 0], hs.at[3, 0], hr.at[1 + 2 * core, 0], sibling, c >= 1)
+    recv(kv.at[2, 1], hs.at[0, 1], hr.at[2, 1], c >= 1)
+    send(kv.at[2, 1], kv.at[0, 1], hs.at[1, 1], hr.at[0, 1], next_chip, jnp.logical_and(c >= 1, c < 15))
+    send(kv.at[2, 1], kv.at[1 + 2 * core, 1], hs.at[3, 1], hr.at[1 + 2 * core, 1], sibling, c >= 1)
+    recv(kv.at[0, 0], hs.at[1, 0], hr.at[0, 0], c >= 2)
+    send(kv.at[0, 0], kv.at[1, 0], hs.at[4, 0], hr.at[1, 0], sibling, jnp.logical_and(c >= 2, core == 1))
+    recv(kv.at[0, 1], hs.at[1, 1], hr.at[0, 1], c >= 2)
+    send(kv.at[0, 1], kv.at[1, 1], hs.at[4, 1], hr.at[1, 1], sibling, jnp.logical_and(c >= 2, core == 1))
     own_ring(OUT)
     on_half(OUT)
     for v in range(2):
@@ -555,13 +570,20 @@
     inverse = np.float32(1.0) / np.float32(10000.0) ** exponent
     inverse = np.concatenate([inverse, inverse])[None, :].astype(np.float32)
     vmem = pl.BlockSpec(memory_space=pltpu.VMEM)
+    hbm = pl.BlockSpec(memory_space=pl.ANY)
     dma = pltpu.SemaphoreType.DMA
     out = pl.pallas_call(
         kernel,
         out_shape=jax.ShapeDtypeStruct((FEAT, TOK), BF16),
-        in_specs=[vmem] * 11,
+        in_specs=[hbm, vmem, vmem, hbm, hbm, hbm, vmem, vmem, hbm, vmem, vmem],
         out_specs=vmem,
         scratch_shapes=[
+            pltpu.VMEM((FEAT, TOK), BF16),
+            pltpu.VMEM((HALF, 256), BF16),
+            pltpu.VMEM((HALF, 128), BF16),
+            pltpu.VMEM((HALF, 128), BF16),
+            pltpu.VMEM((HALF, 256), BF16),
+            dma((5,)),
             pltpu.VMEM((2, 16, FEAT, 128), BF16),
             pltpu.VMEM((16, 2, TOK, HALF), BF16),
             pltpu.VMEM((3, 2, 16, HALF, 256), BF16),

time: 103 us -> 101 us (0.981); the launches traced: 103 us -> 99.4 us
  Pallas kernels: 101 us -> 97.8 us
    pallas_call x1, Pallas kernels: 101 us -> 97.8 us  [body(): pl.pallas_call(kernel, out_shape=jax.ShapeDtypeStruct((FEAT, TOK), BF16),...]
where the time goes in v4:
time: 101 us; the launch traced here: 99.4 us
  Pallas kernels  97.8 us (97%)
  local copies, waits for them, and re-layouts  1.6 us (2%)
    pallas_call x1, Pallas kernels, body(): pl.pallas_call(kernel, out_shape=jax.ShapeDtypeStruct((FEAT, TOK), BF16),...  97.8 us

profile of v4, /device:TPU:6, one launch (start us, length us, event | category | flops | bytes accessed | tf_op | source)
XLA Modules:
  0.0 99.4 jit_solution(13432045141272511729)
XLA Ops:
  0.0 97.8 %shard_map.109 = bf16[336,256]{1,0:T(8,128)(2,1)} custom-call(bf16[336,256]{1,0:T(8,128)(2,1)} %bitcast.8, s32[1,256]{1,0:T(1,128)} %bitcast.11, f32[42,128]{1,0:T(8,128)} %bitcast.10, bf16[168,256]{1,0:T(8,128)(2,1)} %wq_in.1, bf16[168,128]{1,0:T(8,128)(2,1)} %wk_in.1, bf16[168,128]{1,0:T(8,128)(2,1)} %wv_in.1, f32[1,128]{1,0:T(1,128)} %bitcast.12, ...), custom_call_target="tpu_custom_call" | custom-call | flops 3000000000 | bytes 1000000 | tf_op jit(solution)/shard_map/pallas_call | solution.py:575
  97.8 1.6 %copy.13 = bf16[256,336]{0,1:T(8,128)(2,1)} copy(bf16[256,336]{0,1:T(8,128)(2,1)} %bitcast.7) | data formatting | bytes 344064

commit v5 on v4

--- a/solution.py
+++ b/solution.py
@@ -72,6 +72,8 @@
     qs,
     qr,
     loc,
+    ws,
+    wr,
 ):
     s = lax.axis_index("seq")
     t = lax.axis_index("tensor")
@@ -215,6 +217,29 @@
             j = self.slot(2, n)
             recv(self.block(j), xs.at[self.k, n, 2], xr.at[self.k, n, 2])
             return j
+
+    class CrossFlow(TensorFlow):
+        def step_x(self, near):
+            d = 1 - 2 * self.way(0)
+            if near:
+                self.near(0)
+                return lax.rem(4 + d, 4)
+            self.relay_x(0)
+            return lax.rem(4 - d, 4)
+
+        def start_z(self, dx):
+            blk = self.block(self.slot(dx, 0))
+            send(blk, blk, ws.at[dx, 0], wr.at[dx, zl], at_tensor(x, lax.rem(zl + 1, 4)), zl < 3)
+            send(blk, blk, ws.at[dx, 4], wr.at[dx, zl], at_tensor(x, lax.rem(zl + 3, 4)), zl > 0)
+
+        def step_z(self, dx, n):
+            q = near_z(n)
+            blk = self.block(self.slot(dx, n))
+            recv(blk, ws.at[dx, n], wr.at[dx, q])
+            up = q < zl
+            ok = jnp.where(up, zl < 3, zl > 0)
+            dev = at_tensor(x, jnp.where(up, lax.rem(zl + 1, 4), lax.rem(zl + 3, 4)))
+            send(blk, blk, ws.at[dx, n], wr.at[dx, q], dev, ok)
 
     def w_slot(part, way, d):
         half = zh if part == 0 else 1 - zh
@@ -467,9 +492,15 @@
             return carry
 
         lax.fori_loop(0, 2, rows_of, 0)
-        flow = TensorFlow(2 + hd, lambda j, hd=hd: ctx.at[hd, j])
+        if hd == 0:
+            flow = TensorFlow(2, lambda j: ctx.at[0, j, pl.ds(128, 128)])
+            cross = CrossFlow(4, lambda j: ctx.at[0, j, pl.ds(0, 128)])
+        else:
+            flow = TensorFlow(3, lambda j: ctx.at[1, j])
         flow.own_z()
         flow.to_x(0)
+        if hd == 0:
+            cross.to_x(0)
         contexts.append(flow)
 
     oacc[...] = jnp.zeros_like(oacc)
@@ -484,24 +515,39 @@
     on_rings(OUT, 1, 1)
     contexts[0].relay_x(0)
     contexts[0].on_z(1)
+    dx_a = cross.step_x(False)
+    dx_b = cross.step_x(True)
     contexts[1].relay_x(0)
     contexts[1].on_z(1)
+    for dx in (0, dx_a, dx_b):
+        cross.start_z(dx)
     on_rings(OUT, 0, 2)
     on_rings(OUT, 1, 2)
     contexts[0].on_z(2)
+    cross.far(0)
+    cross.start_z(2)
     contexts[0].relay_x(1)
     contexts[1].on_z(2)
     contexts[1].relay_x(1)
+    for dx in (0, dx_a, dx_b):
+        cross.step_z(dx, 1)
     on_rings(OUT, 0, 3)
     on_rings(OUT, 1, 3)
     contexts[0].on_z(3)
     contexts[0].relay_x(2)
     contexts[1].on_z(3)
+    cross.step_z(2, 1)
+    for dx in (0, dx_a):
+        cross.step_z(dx, 2)
     contexts[1].relay_x(2)
+    for dx in (dx_b, 2):
+        cross.step_z(dx, 2)
     on_rings(OUT, 0, 4)
     on_rings(OUT, 1, 4)
     contexts[0].relay_x(3)
     contexts[1].relay_x(3)
+    for dx in (0, dx_a, dx_b, 2):
+        cross.step_z(dx, 3)
 
     def drain():
         for copy, cond in pending:
@@ -598,8 +644,8 @@
             pltpu.VMEM((4, 8, TOK), F32),
             dma((4, 5)),
             dma((4, 4)),
-            dma((4, 4, 3)),
-            dma((4, 4, 3)),
+            dma((5, 4, 3)),
+            dma((5, 4, 3)),
             dma((3, 16)),
             dma((3, 16)),
             dma((3,)),
@@ -613,6 +659,8 @@
             dma((2, 3)),
             dma((2, 4)),
             dma,
+            dma((4, 5)),
+            dma((4, 4)),
         ],
         compiler_params=pltpu.CompilerParams(
             collective_id=0, has_side_effects=True, vmem_limit_bytes=56 << 20

time: 101 us -> 101 us (level)
  no operation moved by 1% of the time
where the time goes in v5:
time: 101 us; the launch traced here: 99.6 us
  Pallas kernels  98 us (97%)
  local copies, waits for them, and re-layouts  1.6 us (2%)
    pallas_call x1, Pallas kernels, body(): pl.pallas_call(kernel, out_shape=jax.ShapeDtypeStruct((FEAT, TOK), BF16),...  98 us

profile of v5, /device:TPU:6, one launch (start us, length us, event | category | flops | bytes accessed | tf_op | source)
XLA Modules:
  0.0 99.6 jit_solution(5382771608546446492)
XLA Ops:
  0.0 98.0 %shard_map.109 = bf16[336,256]{1,0:T(8,128)(2,1)} custom-call(bf16[336,256]{1,0:T(8,128)(2,1)} %bitcast.8, s32[1,256]{1,0:T(1,128)} %bitcast.11, f32[42,128]{1,0:T(8,128)} %bitcast.10, bf16[168,256]{1,0:T(8,128)(2,1)} %wq_in.1, bf16[168,128]{1,0:T(8,128)(2,1)} %wk_in.1, bf16[168,128]{1,0:T(8,128)(2,1)} %wv_in.1, f32[1,128]{1,0:T(1,128)} %bitcast.12, ...), custom_call_target="tpu_custom_call" | custom-call | flops 3000000000 | bytes 1000000 | tf_op jit(solution)/shard_map/pallas_call | solution.py:621
  98.0 1.6 %copy.13 = bf16[256,336]{0,1:T(8,128)(2,1)} copy(bf16[256,336]{0,1:T(8,128)(2,1)} %bitcast.7) | data formatting | bytes 344064
